TPU v7x, 32 devices: a whole 2x2x4 slice. The times are simulated.
32 devices in a mesh: rep: 16 (over z, x, core), ctx: 2 (over y).
Axes of the slice: x: 2, y: 2, z: 4, core: 2. Of those that a mesh axis runs over, the one named last changes fastest.
Arguments:
- activations: bfloat16 [16, 256, 4096], P('rep', 'ctx'), may hold values from -6 to 6
- queries: bfloat16 [16, 256, 2048], P('rep', 'ctx'), may hold values from -110 to 110
- key_states: bfloat16 [16, 256, 512], P('rep', 'ctx'), may hold values from -4 to 4
- targets: bfloat16 [16, 256, 2048], P('rep', 'ctx'), may hold values from -1.5 to 1.5
- value_weight: bfloat16 [16, 4096, 512], P('rep', 'ctx'), may hold values from -5 to 5
- tracker: bfloat16 [16, 4096, 512], P('rep', 'ctx'), may hold values from -5 to 5
- old_gradient: bfloat16 [16, 4096, 512], P('rep', 'ctx'), may hold values from -5 to 5
Outputs:
- new_weight: bfloat16 [16, 4096, 512], P('rep', 'ctx')
- new_tracker: bfloat16 [16, 4096, 512], P('rep', 'ctx')
All inputs are finite; a program needn't handle non-finite values.
Results may differ from a plain program's by a relative error of at most 0.0095.
Values may be sent and summed in bfloat16 or wider, within the bound.
No kernel may reach another device: no remote copies, remote signals or barrier semaphores. Data moves between devices by JAX's collectives and lax.ppermute only.
A program may use at most 64 MiB of HBM per device.

v0:
```python
import jax
import jax.numpy as jnp
from jax import lax
from jax.sharding import PartitionSpec as P

HEADS = 16
KV_HEADS = 4
HEAD_DIM = 128
ROUND = 3


step_size = 0.25
loss_weight = 16.0


def partner(shard, axis, apart):
    return lax.ppermute(shard, axis, [(i, i ^ 1 << apart) for i in range(lax.axis_size(axis))])


def local(activations, queries, key_states, targets, value_weight, tracker, old_gradient):
    token_block = activations[0]
    tokens_here = token_block.shape[0]
    value_scale = token_block.shape[1] ** (-0.5)
    grouping = HEADS // KV_HEADS
    own_weight = value_weight[0]
    weight_full = own_weight.astype(jnp.float32)
    track_full = tracker[0].astype(jnp.float32)
    old_full = old_gradient[0].astype(jnp.float32)
    feature_cols = lax.all_to_all(token_block, "ctx", split_axis=1, concat_axis=0, tiled=True)
    local_values = (
        jnp.dot(
            token_block,
            lax.all_gather(own_weight, "ctx", axis=0, tiled=True),
            preferred_element_type=jnp.float32,
        )
        * value_scale
    ).astype(jnp.bfloat16)
    all_keys, all_values = (
        lax.all_gather(key_states[0], "ctx", axis=0, tiled=True),
        lax.all_gather(local_values, "ctx", axis=0, tiled=True),
    )
    seq_total = all_keys.shape[0]
    query_heads = queries[0].reshape(tokens_here, KV_HEADS, grouping, HEAD_DIM)
    key_heads = all_keys.reshape(seq_total, KV_HEADS, HEAD_DIM)
    value_heads = all_values.reshape(seq_total, KV_HEADS, HEAD_DIM)
    scores = jnp.einsum(
        "ikgd,jkd->kgij", query_heads, key_heads, preferred_element_type=jnp.float32
    ) * HEAD_DIM ** (-0.5)
    query_pos = lax.axis_index("ctx") * tokens_here + jnp.arange(tokens_here)
    key_pos = jnp.arange(seq_total)
    allowed = key_pos[None, :] <= query_pos[:, None]
    scores = jnp.where(allowed, scores, -jnp.inf)
    highest = jnp.max(scores, axis=-1, keepdims=True)
    raised = jnp.exp(scores - highest)
    probabilities = (raised / jnp.sum(raised, axis=-1, keepdims=True)).astype(jnp.bfloat16)
    attended = jnp.einsum(
        "kgij,jkd->ikgd", probabilities, value_heads, preferred_element_type=jnp.float32
    )
    attended = attended.reshape(tokens_here, HEADS * HEAD_DIM)
    out_cot = (loss_weight * (attended - targets[0].astype(jnp.float32))).astype(jnp.bfloat16)
    cot_heads = out_cot.reshape(tokens_here, KV_HEADS, grouping, HEAD_DIM)
    value_terms = jnp.einsum(
        "kgij,ikgd->jkd", probabilities, cot_heads, preferred_element_type=jnp.float32
    )
    value_terms = value_terms.reshape(seq_total, KV_HEADS * HEAD_DIM)
    value_cot16 = lax.psum(value_terms, "ctx").astype(jnp.bfloat16)
    gradient = (
        jnp.einsum("tc,tv->cv", feature_cols, value_cot16, preferred_element_type=jnp.float32)
        * value_scale
    )
    track_half = track_full + gradient - old_full
    moved = weight_full - step_size * track_half
    peer_both = partner(jnp.stack((moved, track_half)), "rep", ROUND)
    new_weight = ((moved + peer_both[0]) * 0.5).astype(jnp.bfloat16)
    new_tracker = ((track_half + peer_both[1]) * 0.5).astype(jnp.bfloat16)
    return (new_weight[None], new_tracker[None])


def solution(mesh):
    return jax.shard_map(
        local,
        mesh=mesh,
        in_specs=(
            P("rep", "ctx", None),
            P("rep", "ctx", None),
            P("rep", "ctx", None),
            P("rep", "ctx", None),
            P("rep", "ctx", None),
            P("rep", "ctx", None),
            P("rep", "ctx", None),
        ),
        out_specs=(P("rep", "ctx", None), P("rep", "ctx", None)),
        check_vma=False,
    )
```

profile of v0, /device:TPU:0, one launch (start us, length us, event | category | flops | bytes accessed | tf_op | source)
XLA Modules:
  0.0 490.4 jit_solution(8389612195669897147)
XLA Ops:
  7.2 0.0 copy-start.2
  7.2 0.0 all-gather.4.cloned.1.call-start
  7.2 0.7 all-gather.4.cloned.1.call-update
  7.9 2.3 copy.36
  10.2 4.2 all-to-all-start
  14.4 0.0 copy-done.2
  14.4 0.1 copy.29
  14.6 25.6 %all-gather.1 = bf16[1,256,512]{1,2,0:T(8,128)(2,1)S(1)} all-gather(bf16[1,128,512]{1,2,0:T(8,128)(2,1)S(1)} %copy.29), channel_id=3, replica_groups=mesh['rep'=16,'ctx'=2] {'ctx'}, dimensions={1}, use_global_device_ids=true | all-gather | bytes 393216 | tf_op jit(solution)/shard_map/all_gather | solution.py:39
  40.2 2.9 copy.27
  43.1 2.2 reshape_squeeze.3
  45.4 2.2 copy.34
  47.6 3.9 copy.28
  51.5 3.9 copy.38
  55.5 3.2 fusion.42
  58.7 0.0 all-to-all-done
  58.7 1.0 copy-done.1
  59.7 1.5 copy.37
  61.2 15.7 %all-gather.4.cloned.1.call-done = bf16[1,4096,512]{2,1,0:T(8,128)(2,1)} async-done(((bf16[1,2048,512]{2,1,0:T(8,128)(2,1)}), bf16[1,4096,512]{2,1,0:T(8,128)(2,1)}) %all-gather.4.cloned.1.call-update) | async-done | bytes 4194320 | tf_op jit(solution)/shard_map/all_gather | solution.py:33
  76.9 3.2 fusion.20
  80.1 6.1 %all_gather.10 = bf16[256,512]{1,0:T(8,128)(2,1)S(1)} all-gather(bf16[128,512]{1,0:T(8,128)(2,1)S(1)} %fusion.20), channel_id=1, replica_groups=mesh['rep'=16,'ctx'=2] {'ctx'}, dimensions={0}, use_global_device_ids=true | all-gather | bytes 393216 | tf_op jit(solution)/shard_map/all_gather | solution.py:40
  86.3 0.8 copy.46
  87.1 4.1 fusion.16
  91.2 16.0 %all-reduce.1 = bf16[256,512]{0,1:T(8,128)(2,1)S(1)} all-reduce(f32[256,512]{0,1:T(8,128)} %bitcast.94), channel_id=1, replica_groups=mesh['rep'=16,'ctx'=2] {'ctx'}, use_global_device_ids=true, to_apply=%region_2.3 | all-reduce | flops 131072 | bytes 786432 | tf_op jit(solution)/shard_map/psum | solution.py:66
  107.2 3.1 convert_subtract_fusion
  110.3 1.0 fusion.9
  111.3 1.1 pad_maximum_fusion
  112.4 2.8 collective-permute-start
  115.2 358.6 %collective-permute-done = f32[2,2048,512]{1,2,0:T(8,128)S(1)} collective-permute-done((f32[2,2048,512]{1,2,0:T(8,128)S(1)}, f32[2,2048,512]{1,2,0:T(8,128)S(1)}, u32[]{:S(2)}, u32[]{:S(2)}) %collective-permute-start) | collective-permute-done | bytes 8388640 | tf_op jit(solution)/shard_map/ppermute | solution.py:17
  473.8 3.2 fusion.11
  477.0 4.1 copy.40
  481.0 0.0 copy-done
  481.0 2.5 copy.39
  (4 shorter events, 0.0 us)
Async XLA Ops:
  7.2 7.3 %copy-start.2 = (bf16[1,128,512]{2,1,0:T(8,128)(2,1)S(1)}, bf16[1,128,512]{2,1,0:T(8,128)(2,1)}, u32[]{:S(2)}) copy-start(bf16[1,128,512]{2,1,0:T(8,128)(2,1)} %param.9) | copy-start | bytes 393220
  7.2 69.7 %all-gather.4.cloned.1.call-start = ((), (), s32[]{:S(2)}) async-start(), calls=%async_computation.1 | async-start | bytes 6291456 | tf_op jit(solution)/shard_map/all_gather | solution.py:33
  10.2 48.5 %all-to-all-start = ((bf16[128,2,2048]{0,2,1:T(8,128)(2,1)}), bf16[128,2,2048]{0,2,1:T(8,128)(2,1)S(1)}, u32[]{:S(2)}, u32[]{:S(2)}) async-start(bf16[128,2,2048]{0,2,1:T(8,128)(2,1)} %bitcast.16), calls=%async_computation | async-start | bytes 2097152 | tf_op jit(solution)/shard_map/all_to_all | solution.py:29
  58.7 1.0 copy-start.1
  112.4 361.4 %collective-permute-start = (f32[2,2048,512]{1,2,0:T(8,128)S(1)}, f32[2,2048,512]{1,2,0:T(8,128)S(1)}, u32[]{:S(2)}, u32[]{:S(2)}) collective-permute-start(f32[2,2048,512]{1,2,0:T(8,128)S(1)} %pad_maximum_fusion), channel_id=1, source_target_pairs={{0,16},{2,18},{4,20},{6,22},{8,24},{10,26},{12,28},{14,30},{16,0},... | collective-permute-start | bytes 25165832 | tf_op jit(solution)/shard_map/ppermute | solution.py:17
  477.0 4.1 copy-start
Sparse Core Ops, SparseCore 0:
  9.6 67.2 all-gather.3
where the time goes:
time: 491 us; the launch traced here: 490 us
  waiting for transfers between devices  375 us (76%)
  blocking collectives  47.7 us (10%)
  local copies, waits for them, and re-layouts  27.5 us (6%)
  between operations  14.1 us (3%)
  matrix products  13.7 us (3%)
  starting transfers between devices  7.11 us (1%)
  other arithmetic  5.27 us (1%)
    ppermute x1, waiting for transfers between devices, partner(): lax.ppermute(shard, axis, [(i, i ^ 1 << apart) for i in range(lax.axis_si...  359 us
    all_gather x1, blocking collectives, local(): lax.all_gather(key_states[0], 'ctx', axis=0, tiled=True)  25.6 us
    unnamed x13, local copies, waits for them, and re-layouts  20.7 us
    psum x1, blocking collectives, local(): value_cot16 = lax.psum(value_terms, 'ctx').astype(jnp.bfloat16)  16 us
    all_gather x1, waiting for transfers between devices, local(): lax.all_gather(own_weight, 'ctx', axis=0, tiled=True)  15.7 us
  transfers between devices with their start and end apart: 3, of which 2 were waited for; matrix products, arithmetic and copies ran while one was open for 5% of the time, Pallas kernels for 0%

commit v1 on v0

v1 whole, which is shorter than its diff:
```python
import functools

import jax
import jax.numpy as jnp
from jax import lax
from jax.experimental import pallas as pl
from jax.experimental.pallas import tpu as pltpu
from jax.sharding import PartitionSpec as P

HEADS = 16
KV_HEADS = 4
HEAD_DIM = 128
ROUND = 3
GROUP = HEADS // KV_HEADS

STEP_SIZE = 0.25
LOSS_WEIGHT = 16.0
CHUNKS = 4
ROWS = 256
VMEM = 32 * 1024 * 1024


def params(**more):
    return pltpu.CompilerParams(vmem_limit_bytes=VMEM, **more)


def shift(block, by):
    n = lax.axis_size("ctx")
    return lax.ppermute(block, "ctx", [(i, (i + by) % n) for i in range(n)])


def partner(block):
    n = lax.axis_size("rep")
    return lax.ppermute(block, "rep", [(i, i ^ 1 << ROUND) for i in range(n)])


def stack_heads(block):
    return jnp.concatenate([block[:, g * HEAD_DIM : (g + 1) * HEAD_DIM] for g in range(GROUP)], axis=0)


def probs_kernel(n, me_ref, q_ref, *refs):
    key_refs, out_ref = refs[:n], refs[n]
    tokens = q_ref.shape[0]
    keys = jnp.concatenate([k[...] for k in key_refs], axis=0)
    scores = lax.dot_general(
        stack_heads(q_ref[...]), keys, (((1,), (1,)), ((), ())), preferred_element_type=jnp.float32
    ) * HEAD_DIM ** (-0.5)
    scores = scores.reshape(GROUP, tokens, n * tokens)
    row = lax.broadcasted_iota(jnp.int32, scores.shape, 1)
    col = lax.broadcasted_iota(jnp.int32, scores.shape, 2)
    last = jnp.where(col < tokens, row, (me_ref[0] + 1) * tokens - 1)
    scores = jnp.where(col <= last, scores, -jnp.inf)
    highest = jnp.max(scores, axis=-1, keepdims=True)
    raised = jnp.exp(scores - highest)
    out_ref[...] = (raised / jnp.sum(raised, axis=-1, keepdims=True)).astype(jnp.bfloat16)


def probabilities(me, queries, keys):
    n, (tokens, _) = len(keys), queries.shape
    return pl.pallas_call(
        functools.partial(probs_kernel, n),
        grid=(KV_HEADS,),
        in_specs=[
            pl.BlockSpec(memory_space=pltpu.SMEM),
            pl.BlockSpec((tokens, GROUP * HEAD_DIM), lambda k: (0, k)),
        ]
        + [pl.BlockSpec((tokens, HEAD_DIM), lambda k: (0, k))] * n,
        out_specs=pl.BlockSpec((GROUP, tokens, n * tokens), lambda k: (k, 0, 0)),
        out_shape=jax.ShapeDtypeStruct((HEADS, tokens, n * tokens), jnp.bfloat16),
        compiler_params=params(),
        cost_estimate=pl.CostEstimate(flops=2 * tokens * tokens * n * HEADS * HEAD_DIM, bytes_accessed=1 << 22, transcendentals=0),
        name="probabilities",
    )(me, queries, *keys)


def terms_kernel(n, probs_ref, target_ref, *refs):
    value_refs, out_refs = refs[:n], refs[n:]
    tokens = target_ref.shape[0]
    probs = probs_ref[...].reshape(GROUP * tokens, n * tokens)
    values = jnp.concatenate([v[...] for v in value_refs], axis=0)
    attended = jnp.dot(probs, values, preferred_element_type=jnp.float32)
    targets = stack_heads(target_ref[...]).astype(jnp.float32)
    cot = (LOSS_WEIGHT * (attended - targets)).astype(jnp.bfloat16)
    terms = lax.dot_general(probs, cot, (((0,), (0,)), ((), ())), preferred_element_type=jnp.float32)
    for s in range(n):
        out_refs[s][...] = terms[s * tokens : (s + 1) * tokens]


def value_terms(probs, targets, values):
    n, (tokens, _) = len(values), targets.shape
    block = pl.BlockSpec((tokens, HEAD_DIM), lambda k: (0, k))
    return pl.pallas_call(
        functools.partial(terms_kernel, n),
        grid=(KV_HEADS,),
        in_specs=[
            pl.BlockSpec((GROUP, tokens, n * tokens), lambda k: (k, 0, 0)),
            pl.BlockSpec((tokens, GROUP * HEAD_DIM), lambda k: (0, k)),
        ]
        + [block] * n,
        out_specs=[block] * n,
        out_shape=[jax.ShapeDtypeStruct((tokens, KV_HEADS * HEAD_DIM), jnp.float32)] * n,
        compiler_params=params(),
        cost_estimate=pl.CostEstimate(flops=4 * tokens * tokens * n * HEADS * HEAD_DIM, bytes_accessed=1 << 22, transcendentals=0),
        name="value_terms",
    )(probs, targets, *values)


def tracker_kernel(n, scale, track_ref, old_ref, *refs):
    feature_refs, cot_refs, (wide_ref, sent_ref) = refs[:n], refs[n : 2 * n], refs[2 * n : 2 * n + 2]
    gradient = sum(
        lax.dot_general(f[...], c[...], (((0,), (0,)), ((), ())), preferred_element_type=jnp.float32)
        for f, c in zip(feature_refs, cot_refs)
    )
    half = track_ref[...].astype(jnp.float32) + gradient * scale - old_ref[...].astype(jnp.float32)
    wide_ref[...] = half
    sent_ref[...] = half.astype(jnp.bfloat16)


def tracker_chunk(chunk, rows, scale, track, old, features, cots, after):
    n, (tokens, _) = len(features), features[0].shape
    cols = track.shape[1]
    step = min(ROWS, rows)
    first = chunk * (rows // step)
    moving = pl.BlockSpec((step, cols), lambda i: (first + i, 0))
    own = pl.BlockSpec((step, cols), lambda i: (i, 0))
    return pl.pallas_call(
        functools.partial(tracker_kernel, n, scale),
        grid=(rows // step,),
        in_specs=[moving, moving]
        + [pl.BlockSpec((tokens, step), lambda i: (0, first + i))] * n
        + [pl.BlockSpec((tokens, cols), lambda i: (0, 0))] * n,
        out_specs=[own, own],
        out_shape=[
            jax.ShapeDtypeStruct((rows, cols), jnp.float32),
            jax.ShapeDtypeStruct((rows, cols), jnp.bfloat16),
        ],
        compiler_params=params(),
        cost_estimate=pl.CostEstimate(flops=2 * rows * tokens * n * cols, bytes_accessed=10 * rows * cols, transcendentals=0),
        name="tracker_half",
    )(track, old, *features, *cots)


def mix_kernel(weight_ref, peer_weight_ref, half_ref, peer_half_ref, *refs):
    new_weight_ref, new_tracker_ref = refs[-2:]
    both = half_ref[...] + peer_half_ref[...].astype(jnp.float32)
    weights = weight_ref[...].astype(jnp.float32) + peer_weight_ref[...].astype(jnp.float32)
    new_weight_ref[...] = ((weights - STEP_SIZE * both) * 0.5).astype(jnp.bfloat16)
    new_tracker_ref[...] = (both * 0.5).astype(jnp.bfloat16)


def mix_chunk(chunk, weight, peer_weight, half, peer_half, outs):
    rows, cols = half.shape
    step = min(ROWS, rows)
    first = chunk * (rows // step)
    moving = pl.BlockSpec((step, cols), lambda i: (first + i, 0))
    own = pl.BlockSpec((step, cols), lambda i: (i, 0))
    return pl.pallas_call(
        mix_kernel,
        grid=(rows // step,),
        in_specs=[moving, moving, own, own] + [pl.BlockSpec(memory_space=pl.ANY)] * len(outs),
        out_specs=[moving, moving],
        out_shape=[jax.ShapeDtypeStruct(weight.shape, jnp.bfloat16)] * 2,
        input_output_aliases={4 + i: i for i in range(len(outs))},
        compiler_params=params(),
        cost_estimate=pl.CostEstimate(flops=5 * rows * cols, bytes_accessed=14 * rows * cols, transcendentals=0),
        name="mix",
    )(weight, peer_weight, half, peer_half, *outs)


def local(activations, queries, key_states, targets, value_weight, tracker, old_gradient):
    n, me = lax.axis_size("ctx"), lax.axis_index("ctx")
    tokens, width = activations.shape[1:]
    scale = width ** (-0.5)
    depth = width // n
    weight = value_weight[0]
    peer_weight = partner(weight)

    columns = [lax.dynamic_slice_in_dim(activations[0], (me + s) % n * depth, depth, axis=1) for s in range(n)]
    features = [columns[0]] + [shift(columns[s], s) for s in range(1, n)]
    keys = [key_states[0]] + [shift(key_states[0], s) for s in range(1, n)]
    probs = probabilities(me.astype(jnp.int32).reshape(1), queries[0], keys)

    parts = [jnp.dot(f, weight, preferred_element_type=jnp.float32) for f in features]
    own = parts[0] + sum(shift(parts[s], -s) for s in range(1, n))
    own_values = (own * scale).astype(jnp.bfloat16)
    values = [own_values] + [shift(own_values, s) for s in range(1, n)]

    terms = value_terms(probs, targets[0], values)
    own_cot = (terms[0] + sum(shift(terms[s], -s) for s in range(1, n))).astype(jnp.bfloat16)
    cots = [own_cot] + [shift(own_cot, s) for s in range(1, n)]

    rows = depth // CHUNKS
    outs = ()
    for c in range(CHUNKS):
        half, sent = tracker_chunk(c, rows, scale, tracker[0], old_gradient[0], features, cots, None)
        outs = mix_chunk(c, weight, peer_weight, half, partner(sent), outs)
    return outs[0][None], outs[1][None]


def solution(mesh):
    spec = P("rep", "ctx", None)
    return jax.shard_map(
        local,
        mesh=mesh,
        in_specs=(spec,) * 7,
        out_specs=(spec, spec),
        check_vma=False,
    )
```

time: 491 us -> 189 us (0.38)
  waiting for transfers between devices: 375 us -> 155 us
  blocking collectives: 47.7 us -> 0 us
  local copies, waits for them, and re-layouts: 27.5 us -> 1.48 us
  between operations: 14.1 us -> 0.79 us
  matrix products: 13.7 us -> 0.89 us
  starting transfers between devices: 7.11 us -> 19.8 us
  Pallas kernels: 0 us -> 11.5 us
  other arithmetic: 5.27 us -> 0.08 us
    ppermute x1 -> x11, waiting for transfers between devices: 359 us -> 155 us  [the longest x5 130 us: partner(): return lax.ppermute(block, 'rep', [(i, i ^ 1 << ROUND) for i in range(n)])]
    all_gather x2 -> x0, blocking collectives: 31.7 us -> none  [the longest x1 25.6 us: local(): lax.all_gather(key_states[0], 'ctx', axis=0, tiled=True)]
    unnamed x13 -> x12, local copies, waits for them, and re-layouts: 20.7 us -> 0.03 us
    ppermute x1 -> x11, starting transfers between devices: 2.84 us -> 19.8 us  [the longest x6 10.6 us: shift(): return lax.ppermute(block, 'ctx', [(i, (i + by) % n) for i in range(n)])]
    psum x1 -> x0, blocking collectives: 16 us -> none  [local(): value_cot16 = lax.psum(value_terms, 'ctx').astype(jnp.bfloat16)]
    all_gather x1 -> x0, waiting for transfers between devices: 15.7 us -> none  [local(): lax.all_gather(own_weight, 'ctx', axis=0, tiled=True)]
    pallas_call x0 -> x10, Pallas kernels: none -> 11.5 us  [the longest x4 4.51 us: mix_chunk(): pl.pallas_call(mix_kernel, grid=(rows // step,), in_specs=[moving, moving...]
    dot_general x3 -> x2, matrix products: 10.5 us -> 0.89 us  [local(): jnp.dot(f, weight, preferred_element_type=jnp.float32)]
  transfers between devices with their start and end apart: 3 -> 11, of which waited for: 2 -> 9; matrix products, arithmetic and copies ran while one was open for 5% -> 1% of each run, Pallas kernels for 0% -> 5%
where the time goes in v1:
time: 189 us
  waiting for transfers between devices  155 us (82%)
  starting transfers between devices  19.8 us (10%)
  Pallas kernels  11.5 us (6%)
    ppermute x5, waiting for transfers between devices, partner(): return lax.ppermute(block, 'rep', [(i, i ^ 1 << ROUND) for i in range(n)])  130 us
    ppermute x6, waiting for transfers between devices, shift(): return lax.ppermute(block, 'ctx', [(i, (i + by) % n) for i in range(n)])  24.9 us
    ppermute x6, starting transfers between devices, shift(): return lax.ppermute(block, 'ctx', [(i, (i + by) % n) for i in range(n)])  10.6 us
    ppermute x5, starting transfers between devices, partner(): return lax.ppermute(block, 'rep', [(i, i ^ 1 << ROUND) for i in range(n)])  9.12 us
    pallas_call x4, Pallas kernels, mix_chunk(): pl.pallas_call(mix_kernel, grid=(rows // step,), in_specs=[moving, moving...  4.51 us
  transfers between devices with their start and end apart: 11, of which 9 were waited for; matrix products, arithmetic and copies ran while one was open for 1% of the time, Pallas kernels for 5%

profile of v1, /device:TPU:0, one launch (start us, length us, event | category | flops | bytes accessed | tf_op | source)
XLA Modules:
  0.0 189.3 jit_solution(16191570120192960140)
XLA Ops:
  0.7 1.4 dynamic-slice_bitcast_fusion
  2.1 3.0 %collective-permute-start.1 = (bf16[128,2048]{1,0:T(8,128)(2,1)S(1)}, bf16[128,2048]{1,0:T(8,128)(2,1)S(1)}, u32[]{:S(2)}, u32[]{:S(2)}) collective-permute-start(bf16[128,2048]{1,0:T(8,128)(2,1)S(1)} %get-tuple-element.38), channel_id=1, source_target_pairs={{0,1},{1,0},{2,3},{3,2},{4,5},{5,4},{6,7},{7,6},{8,9},{9,8},{10,11... | collective-permute-start | bytes 1572872 | tf_op jit(solution)/shard_map/ppermute | solution.py:29
  5.2 3.0 %collective-permute-start = (bf16[2048,512]{1,0:T(8,128)(2,1)S(1)}, bf16[2048,512]{1,0:T(8,128)(2,1)S(1)}, u32[]{:S(2)}, u32[]{:S(2)}) collective-permute-start(bf16[2048,512]{1,0:T(8,128)(2,1)S(1)} %bitcast.19), channel_id=1, source_target_pairs={{0,16},{2,18},{4,20},{6,22},{8,24},{10,26},{12,28},{14,30},{16,0},... | collective-permute-start | bytes 6291464 | tf_op jit(solution)/shard_map/ppermute | solution.py:34
  8.3 9.7 %collective-permute-done.1.refs_1_ = bf16[128,2048]{1,0:T(8,128)(2,1)S(1)} collective-permute-done((bf16[128,2048]{1,0:T(8,128)(2,1)S(1)}, bf16[128,2048]{1,0:T(8,128)(2,1)S(1)}, u32[]{:S(2)}, u32[]{:S(2)}) %collective-permute-start.1) | collective-permute-done | bytes 524320 | tf_op jit(solution)/shard_map/ppermute | solution.py:29
  17.9 0.4 fusion
  18.4 2.1 %collective-permute-start.3 = (f32[128,512]{1,0:T(8,128)S(1)}, f32[128,512]{1,0:T(8,128)S(1)}, u32[]{:S(2)}, u32[]{:S(2)}) collective-permute-start(f32[128,512]{1,0:T(8,128)S(1)} %fusion), channel_id=1, source_target_pairs={{0,1},{1,0},{2,3},{3,2},{4,5},{5,4},{6,7},{7,6},{8,9},{9,8},{10,11... | collective-permute-start | bytes 786440 | tf_op jit(solution)/shard_map/ppermute | solution.py:29
  20.5 0.4 fusion.2
  21.0 4.5 %collective-permute-done.3 = f32[128,512]{1,0:T(8,128)S(1)} collective-permute-done((f32[128,512]{1,0:T(8,128)S(1)}, f32[128,512]{1,0:T(8,128)S(1)}, u32[]{:S(2)}, u32[]{:S(2)}) %collective-permute-start.3) | collective-permute-done | bytes 262176 | tf_op jit(solution)/shard_map/ppermute | solution.py:29
  25.5 1.8 collective-permute-start.4
  27.4 1.8 probabilities.1.probs_ref
  29.2 1.4 collective-permute-done.4.refs_1_
  30.6 2.1 %value_terms.1 = (f32[128,512]{1,0:T(8,128)S(1)}, f32[128,512]{1,0:T(8,128)S(1)}) custom-call(bf16[16,128,256]{2,1,0:T(8,128)(2,1)S(1)} %probabilities.1.probs_ref, bf16[128,2048]{1,0:T(8,128)(2,1)S(1)} %bitcast.32, bf16[128,512]{1,0:T(8,128)(2,1)S(1)} %multiply_convert_fusion.refs_0_, bf16[128,512]{1,0:T(8,128)(2,1)S(1)} %collective-permute-done.4.refs_1_), custom_call_target="tpu_custom_call" | custom-call | flops 268435456 | bytes 4194304 | tf_op jit(solution)/shard_map/value_terms/pallas_call | solution.py:92
  32.7 1.8 collective-permute-start.5
  34.5 6.0 %collective-permute-done.5 = f32[128,512]{1,0:T(8,128)S(1)} collective-permute-done((f32[128,512]{1,0:T(8,128)S(1)}, f32[128,512]{1,0:T(8,128)S(1)}, u32[]{:S(2)}, u32[]{:S(2)}) %collective-permute-start.5) | collective-permute-done | bytes 262176 | tf_op jit(solution)/shard_map/ppermute | solution.py:29
  40.6 1.8 collective-permute-start.6
  42.4 3.2 %collective-permute-done.6.refs_3_ = bf16[128,512]{1,0:T(8,128)(2,1)S(1)} collective-permute-done((bf16[128,512]{1,0:T(8,128)(2,1)S(1)}, bf16[128,512]{1,0:T(8,128)(2,1)S(1)}, u32[]{:S(2)}, u32[]{:S(2)}) %collective-permute-start.6) | collective-permute-done | bytes 131104 | tf_op jit(solution)/shard_map/ppermute | solution.py:29
  45.6 0.8 tracker_half.7
  46.4 2.8 %collective-permute-start.10 = (bf16[512,512]{1,0:T(8,128)(2,1)S(1)}, bf16[512,512]{1,0:T(8,128)(2,1)S(1)}, u32[]{:S(2)}, u32[]{:S(2)}) collective-permute-start(bf16[512,512]{1,0:T(8,128)(2,1)S(1)} %get-tuple-element.29), channel_id=1, source_target_pairs={{0,16},{2,18},{4,20},{6,22},{8,24},{10,26},{12,28},{14,30},{16,0},... | collective-permute-start | bytes 1572872 | tf_op jit(solution)/shard_map/ppermute | solution.py:34
  49.2 0.8 tracker_half.6
  50.0 0.2 collective-permute-start.9
  50.2 0.8 tracker_half.5
  51.0 2.8 %collective-permute-start.8 = (bf16[512,512]{1,0:T(8,128)(2,1)S(1)}, bf16[512,512]{1,0:T(8,128)(2,1)S(1)}, u32[]{:S(2)}, u32[]{:S(2)}) collective-permute-start(bf16[512,512]{1,0:T(8,128)(2,1)S(1)} %get-tuple-element.25), channel_id=1, source_target_pairs={{0,16},{2,18},{4,20},{6,22},{8,24},{10,26},{12,28},{14,30},{16,0},... | collective-permute-start | bytes 1572872 | tf_op jit(solution)/shard_map/ppermute | solution.py:34
  53.8 0.8 tracker_half.4
  54.6 0.2 collective-permute-start.7
  54.9 100.8 %collective-permute-done.10.peer_half_ref = bf16[512,512]{1,0:T(8,128)(2,1)S(1)} collective-permute-done((bf16[512,512]{1,0:T(8,128)(2,1)S(1)}, bf16[512,512]{1,0:T(8,128)(2,1)S(1)}, u32[]{:S(2)}, u32[]{:S(2)}) %collective-permute-start.10) | collective-permute-done | bytes 524320 | tf_op jit(solution)/shard_map/ppermute | solution.py:34
  155.7 1.1 mix.4
  156.8 10.1 %collective-permute-done.9.peer_half_ref = bf16[512,512]{1,0:T(8,128)(2,1)S(1)} collective-permute-done((bf16[512,512]{1,0:T(8,128)(2,1)S(1)}, bf16[512,512]{1,0:T(8,128)(2,1)S(1)}, u32[]{:S(2)}, u32[]{:S(2)}) %collective-permute-start.9) | collective-permute-done | bytes 524320 | tf_op jit(solution)/shard_map/ppermute | solution.py:34
  166.9 1.1 mix.5
  168.0 10.1 %collective-permute-done.8.peer_half_ref = bf16[512,512]{1,0:T(8,128)(2,1)S(1)} collective-permute-done((bf16[512,512]{1,0:T(8,128)(2,1)S(1)}, bf16[512,512]{1,0:T(8,128)(2,1)S(1)}, u32[]{:S(2)}, u32[]{:S(2)}) %collective-permute-start.8) | collective-permute-done | bytes 524320 | tf_op jit(solution)/shard_map/ppermute | solution.py:34
  178.1 1.1 mix.6
  179.3 8.9 %collective-permute-done.7.peer_half_ref = bf16[512,512]{1,0:T(8,128)(2,1)S(1)} collective-permute-done((bf16[512,512]{1,0:T(8,128)(2,1)S(1)}, bf16[512,512]{1,0:T(8,128)(2,1)S(1)}, u32[]{:S(2)}, u32[]{:S(2)}) %collective-permute-start.7) | collective-permute-done | bytes 524320 | tf_op jit(solution)/shard_map/ppermute | solution.py:34
  188.1 1.1 mix.7
  (17 shorter events, 0.2 us)
Async XLA Ops:
  0.6 4.6 %copy-start = (bf16[1,2048,512]{2,1,0:T(8,128)(2,1)S(1)}, bf16[1,2048,512]{2,1,0:T(8,128)(2,1)}, u32[]{:S(2)}) copy-start(bf16[1,2048,512]{2,1,0:T(8,128)(2,1)} %param.11) | copy-start | bytes 6291460
  2.1 15.8 %collective-permute-start.1 = (bf16[128,2048]{1,0:T(8,128)(2,1)S(1)}, bf16[128,2048]{1,0:T(8,128)(2,1)S(1)}, u32[]{:S(2)}, u32[]{:S(2)}) collective-permute-start(bf16[128,2048]{1,0:T(8,128)(2,1)S(1)} %get-tuple-element.38), channel_id=1, source_target_pairs={{0,1},{1,0},{2,3},{3,2},{4,5},{5,4},{6,7},{7,6},{8,9},{9,8},{10,11... | collective-permute-start | bytes 1572872 | tf_op jit(solution)/shard_map/ppermute | solution.py:29
  5.2 22.2 %collective-permute-start.2 = (bf16[128,512]{1,0:T(8,128)(2,1)}, bf16[128,512]{1,0:T(8,128)(2,1)S(1)}, u32[]{:S(2)}, u32[]{:S(2)}) collective-permute-start(bf16[128,512]{1,0:T(8,128)(2,1)} %bitcast.34), channel_id=1, source_target_pairs={{0,1},{1,0},{2,3},{3,2},{4,5},{5,4},{6,7},{7,6},{8,9},{9,8},{10,11... | collective-permute-start | bytes 393224 | tf_op jit(solution)/shard_map/ppermute | solution.py:29
  5.2 150.4 %collective-permute-start = (bf16[2048,512]{1,0:T(8,128)(2,1)S(1)}, bf16[2048,512]{1,0:T(8,128)(2,1)S(1)}, u32[]{:S(2)}, u32[]{:S(2)}) collective-permute-start(bf16[2048,512]{1,0:T(8,128)(2,1)S(1)} %bitcast.19), channel_id=1, source_target_pairs={{0,16},{2,18},{4,20},{6,22},{8,24},{10,26},{12,28},{14,30},{16,0},... | collective-permute-start | bytes 6291464 | tf_op jit(solution)/shard_map/ppermute | solution.py:34
  18.4 9.0 %copy-start.4 = (bf16[1,128,2048]{2,1,0:T(8,128)(2,1)S(1)}, bf16[1,128,2048]{2,1,0:T(8,128)(2,1)}, u32[]{:S(2)}) copy-start(bf16[1,128,2048]{2,1,0:T(8,128)(2,1)} %param.8) | copy-start | bytes 1572868
  18.4 9.0 %copy-start.5 = (bf16[1,128,512]{2,1,0:T(8,128)(2,1)S(1)}, bf16[1,128,512]{2,1,0:T(8,128)(2,1)}, u32[]{:S(2)}) copy-start(bf16[1,128,512]{2,1,0:T(8,128)(2,1)} %param.9) | copy-start | bytes 393220
  18.4 7.1 %collective-permute-start.3 = (f32[128,512]{1,0:T(8,128)S(1)}, f32[128,512]{1,0:T(8,128)S(1)}, u32[]{:S(2)}, u32[]{:S(2)}) collective-permute-start(f32[128,512]{1,0:T(8,128)S(1)} %fusion), channel_id=1, source_target_pairs={{0,1},{1,0},{2,3},{3,2},{4,5},{5,4},{6,7},{7,6},{8,9},{9,8},{10,11... | collective-permute-start | bytes 786440 | tf_op jit(solution)/shard_map/ppermute | solution.py:29
  20.5 10.1 %copy-start.3 = (bf16[1,128,2048]{2,1,0:T(8,128)(2,1)S(1)}, bf16[1,128,2048]{2,1,0:T(8,128)(2,1)}, u32[]{:S(2)}) copy-start(bf16[1,128,2048]{2,1,0:T(8,128)(2,1)} %param.10) | copy-start | bytes 1572868
  25.5 5.0 %collective-permute-start.4 = (bf16[128,512]{1,0:T(8,128)(2,1)S(1)}, bf16[128,512]{1,0:T(8,128)(2,1)S(1)}, u32[]{:S(2)}, u32[]{:S(2)}) collective-permute-start(bf16[128,512]{1,0:T(8,128)(2,1)S(1)} %multiply_convert_fusion.refs_0_), channel_id=1, source_target_pairs={{0,1},{1,0},{2,3},{3,2},{4,5},{5,4},{6,7},{7,6},{8,9},{9,8},{10,11... | collective-permute-start | bytes 393224 | tf_op jit(solution)/shard_map/ppermute | solution.py:29
  27.4 18.2 %copy-start.1 = (bf16[1,2048,512]{2,1,0:T(8,128)(2,1)S(1)}, bf16[1,2048,512]{2,1,0:T(8,128)(2,1)}, u32[]{:S(2)}) copy-start(bf16[1,2048,512]{2,1,0:T(8,128)(2,1)} %param.12) | copy-start | bytes 6291460
  27.4 18.2 %copy-start.2 = (bf16[1,2048,512]{2,1,0:T(8,128)(2,1)S(1)}, bf16[1,2048,512]{2,1,0:T(8,128)(2,1)}, u32[]{:S(2)}) copy-start(bf16[1,2048,512]{2,1,0:T(8,128)(2,1)} %param.13) | copy-start | bytes 6291460
  32.7 7.8 %collective-permute-start.5 = (f32[128,512]{1,0:T(8,128)S(1)}, f32[128,512]{1,0:T(8,128)S(1)}, u32[]{:S(2)}, u32[]{:S(2)}) collective-permute-start(f32[128,512]{1,0:T(8,128)S(1)} %get-tuple-element.21), channel_id=1, source_target_pairs={{0,1},{1,0},{2,3},{3,2},{4,5},{5,4},{6,7},{7,6},{8,9},{9,8},{10,11... | collective-permute-start | bytes 786440 | tf_op jit(solution)/shard_map/ppermute | solution.py:29
  40.6 5.0 %collective-permute-start.6 = (bf16[128,512]{1,0:T(8,128)(2,1)S(1)}, bf16[128,512]{1,0:T(8,128)(2,1)S(1)}, u32[]{:S(2)}, u32[]{:S(2)}) collective-permute-start(bf16[128,512]{1,0:T(8,128)(2,1)S(1)} %add_convert_fusion.refs_2_), channel_id=1, source_target_pairs={{0,1},{1,0},{2,3},{3,2},{4,5},{5,4},{6,7},{7,6},{8,9},{9,8},{10,11... | collective-permute-start | bytes 393224 | tf_op jit(solution)/shard_map/ppermute | solution.py:29
  46.4 109.3 %collective-permute-start.10 = (bf16[512,512]{1,0:T(8,128)(2,1)S(1)}, bf16[512,512]{1,0:T(8,128)(2,1)S(1)}, u32[]{:S(2)}, u32[]{:S(2)}) collective-permute-start(bf16[512,512]{1,0:T(8,128)(2,1)S(1)} %get-tuple-element.29), channel_id=1, source_target_pairs={{0,16},{2,18},{4,20},{6,22},{8,24},{10,26},{12,28},{14,30},{16,0},... | collective-permute-start | bytes 1572872 | tf_op jit(solution)/shard_map/ppermute | solution.py:34
  50.0 116.9 %collective-permute-start.9 = (bf16[512,512]{1,0:T(8,128)(2,1)S(1)}, bf16[512,512]{1,0:T(8,128)(2,1)S(1)}, u32[]{:S(2)}, u32[]{:S(2)}) collective-permute-start(bf16[512,512]{1,0:T(8,128)(2,1)S(1)} %get-tuple-element.27), channel_id=1, source_target_pairs={{0,16},{2,18},{4,20},{6,22},{8,24},{10,26},{12,28},{14,30},{16,0},... | collective-permute-start | bytes 1572872 | tf_op jit(solution)/shard_map/ppermute | solution.py:34
  51.0 127.1 %collective-permute-start.8 = (bf16[512,512]{1,0:T(8,128)(2,1)S(1)}, bf16[512,512]{1,0:T(8,128)(2,1)S(1)}, u32[]{:S(2)}, u32[]{:S(2)}) collective-permute-start(bf16[512,512]{1,0:T(8,128)(2,1)S(1)} %get-tuple-element.25), channel_id=1, source_target_pairs={{0,16},{2,18},{4,20},{6,22},{8,24},{10,26},{12,28},{14,30},{16,0},... | collective-permute-start | bytes 1572872 | tf_op jit(solution)/shard_map/ppermute | solution.py:34
  54.6 133.5 %collective-permute-start.7 = (bf16[512,512]{1,0:T(8,128)(2,1)S(1)}, bf16[512,512]{1,0:T(8,128)(2,1)S(1)}, u32[]{:S(2)}, u32[]{:S(2)}) collective-permute-start(bf16[512,512]{1,0:T(8,128)(2,1)S(1)} %get-tuple-element.23), channel_id=1, source_target_pairs={{0,16},{2,18},{4,20},{6,22},{8,24},{10,26},{12,28},{14,30},{16,0},... | collective-permute-start | bytes 1572872 | tf_op jit(solution)/shard_map/ppermute | solution.py:34

commit v2 on v1

--- a/solution.py
+++ b/solution.py
@@ -175,19 +175,27 @@
     weight = value_weight[0]
     peer_weight = partner(weight)
 
-    columns = [lax.dynamic_slice_in_dim(activations[0], (me + s) % n * depth, depth, axis=1) for s in range(n)]
-    features = [columns[0]] + [shift(columns[s], s) for s in range(1, n)]
-    keys = [key_states[0]] + [shift(key_states[0], s) for s in range(1, n)]
-    probs = probabilities(me.astype(jnp.int32).reshape(1), queries[0], keys)
-
-    parts = [jnp.dot(f, weight, preferred_element_type=jnp.float32) for f in features]
-    own = parts[0] + sum(shift(parts[s], -s) for s in range(1, n))
-    own_values = (own * scale).astype(jnp.bfloat16)
-    values = [own_values] + [shift(own_values, s) for s in range(1, n)]
-
-    terms = value_terms(probs, targets[0], values)
-    own_cot = (terms[0] + sum(shift(terms[s], -s) for s in range(1, n))).astype(jnp.bfloat16)
-    cots = [own_cot] + [shift(own_cot, s) for s in range(1, n)]
+    def chain():
+        columns = [lax.dynamic_slice_in_dim(activations[0], (me + s) % n * depth, depth, axis=1) for s in range(n)]
+        features = [columns[0]] + [shift(columns[s], s) for s in range(1, n)]
+        keys = [key_states[0]] + [shift(key_states[0], s) for s in range(1, n)]
+        probs = probabilities(me.astype(jnp.int32).reshape(1), queries[0], keys)
+
+        parts = [jnp.dot(f, weight, preferred_element_type=jnp.float32) for f in features]
+        own = parts[0] + sum(shift(parts[s], -s) for s in range(1, n))
+        own_values = (own * scale).astype(jnp.bfloat16)
+        values = [own_values] + [shift(own_values, s) for s in range(1, n)]
+
+        terms = value_terms(probs, targets[0], values)
+        own_cot = (terms[0] + sum(shift(terms[s], -s) for s in range(1, n))).astype(jnp.bfloat16)
+        cots = [own_cot] + [shift(own_cot, s) for s in range(1, n)]
+        return features, cots
+
+    def never():
+        shapes = jax.eval_shape(chain)
+        return jax.tree.map(lambda x: jnp.zeros(x.shape, x.dtype), shapes)
+
+    features, cots = lax.cond(me < n, chain, never)
 
     rows = depth // CHUNKS
     outs = ()

time: 189 us -> 187 us (0.989)
  waiting for transfers between devices: 155 us -> 145 us
  Pallas kernels: 11.5 us -> 15.4 us
  local copies, waits for them, and re-layouts: 1.48 us -> 4.66 us
    ppermute x5, waiting for transfers between devices: 130 us -> 117 us  [partner(): return lax.ppermute(block, 'rep', [(i, i ^ 1 << ROUND) for i in range(n)])]
    pallas_call x4, Pallas kernels: 3.13 us -> 7.04 us  [tracker_chunk(): pl.pallas_call(functools.partial(tracker_kernel, n, scale), grid=(rows //...]
    unnamed x12 -> x6, local copies, waits for them, and re-layouts: 0.03 us -> 3.19 us
    ppermute x6, waiting for transfers between devices: 24.9 us -> 27.8 us  [shift(): return lax.ppermute(block, 'ctx', [(i, (i + by) % n) for i in range(n)])]
  transfers between devices with their start and end apart: 11 -> 11, of which waited for: 9 -> 9; matrix products, arithmetic and copies ran while one was open for 1% -> 2% of each run, Pallas kernels for 5% -> 8%
where the time goes in v2:
time: 187 us
  waiting for transfers between devices  145 us (78%)
  starting transfers between devices  19 us (10%)
  Pallas kernels  15.4 us (8%)
  local copies, waits for them, and re-layouts  4.66 us (2%)
    ppermute x5, waiting for transfers between devices, partner(): return lax.ppermute(block, 'rep', [(i, i ^ 1 << ROUND) for i in range(n)])  117 us
    ppermute x6, waiting for transfers between devices, shift(): return lax.ppermute(block, 'ctx', [(i, (i + by) % n) for i in range(n)])  27.8 us
    ppermute x5, starting transfers between devices, partner(): return lax.ppermute(block, 'rep', [(i, i ^ 1 << ROUND) for i in range(n)])  10.1 us
    ppermute x6, starting transfers between devices, shift(): return lax.ppermute(block, 'ctx', [(i, (i + by) % n) for i in range(n)])  8.95 us
    pallas_call x4, Pallas kernels, tracker_chunk(): pl.pallas_call(functools.partial(tracker_kernel, n, scale), grid=(rows //...  7.04 us
    pallas_call x4, Pallas kernels, mix_chunk(): pl.pallas_call(mix_kernel, grid=(rows // step,), in_specs=[moving, moving...  4.53 us
  transfers between devices with their start and end apart: 11, of which 9 were waited for; matrix products, arithmetic and copies ran while one was open for 2% of the time, Pallas kernels for 8%

profile of v2, /device:TPU:0, one launch (start us, length us, event | category | flops | bytes accessed | tf_op | source)
XLA Modules:
  0.0 186.5 jit_solution(10205026945347856659)
XLA Ops:
  0.6 4.1 %collective-permute-start.6 = (bf16[2048,512]{1,0:T(8,128)(2,1)}, bf16[2048,512]{1,0:T(8,128)(2,1)S(1)}, u32[]{:S(2)}, u32[]{:S(2)}) collective-permute-start(bf16[2048,512]{1,0:T(8,128)(2,1)} %bitcast.25), channel_id=1, source_target_pairs={{0,16},{2,18},{4,20},{6,22},{8,24},{10,26},{12,28},{14,30},{16,0},... | collective-permute-start | bytes 6291464 | tf_op jit(solution)/shard_map/ppermute | solution.py:34
  4.7 43.8 %conditional.1 = (bf16[128,2048]{1,0:T(8,128)(2,1)S(1)}, bf16[128,2048]{1,0:T(8,128)(2,1)S(1)}, bf16[128,512]{1,0:T(8,128)(2,1)}, bf16[128,512]{1,0:T(8,128)(2,1)}) conditional(s32[]{:T(128)} %convert_element_type.9, () %tuple.16, (s32[]{:T(128)}, bf16[1,128,4096]{2,1,0:T(8,128)(2,1)}, bf16[1,128,2048]{2,1,0:T(8,128)(2,1)}, ...), branch_computations={%region_0.0_spmd, %region_1.2_spmd} | conditional | flops 939851776 | bytes 44827448 | solution.py:198
  4.7 1.4 dynamic-slice_bitcast_fusion
  6.2 1.6 collective-permute-start
  8.3 12.8 %collective-permute-done = bf16[128,2048]{1,0:T(8,128)(2,1)S(1)} collective-permute-done((bf16[128,2048]{1,0:T(8,128)(2,1)S(1)}, bf16[128,2048]{1,0:T(8,128)(2,1)S(1)}, u32[]{:S(2)}, u32[]{:S(2)}) %collective-permute-start) | collective-permute-done | bytes 524320 | tf_op jit(solution)/shard_map/cond/branch_1_fun/ppermute | solution.py:29
  21.5 1.6 collective-permute-start.2
  23.6 4.5 %collective-permute-done.2 = f32[128,512]{1,0:T(8,128)S(1)} collective-permute-done((f32[128,512]{1,0:T(8,128)S(1)}, f32[128,512]{1,0:T(8,128)S(1)}, u32[]{:S(2)}, u32[]{:S(2)}) %collective-permute-start.2) | collective-permute-done | bytes 262176 | tf_op jit(solution)/shard_map/cond/branch_1_fun/ppermute | solution.py:29
  28.1 1.6 collective-permute-start.3
  29.7 1.8 probabilities.1.probs_ref
  31.5 1.6 collective-permute-done.3.refs_1_
  33.1 2.1 %value_terms.1 = (f32[128,512]{1,0:T(8,128)S(1)}, f32[128,512]{1,0:T(8,128)S(1)}) custom-call(bf16[16,128,256]{2,1,0:T(8,128)(2,1)S(1)} %probabilities.1.probs_ref, bf16[128,2048]{1,0:T(8,128)(2,1)S(1)} %bitcast.33, bf16[128,512]{1,0:T(8,128)(2,1)S(1)} %multiply_convert_fusion.refs_0_, bf16[128,512]{1,0:T(8,128)(2,1)S(1)} %collective-permute-done.3.refs_1_), custom_call_target="tpu_custom_call" | custom-call | flops 268435456 | bytes 4194304 | tf_op jit(solution)/shard_map/cond/branch_1_fun/value_terms/pallas_call | solution.py:92
  35.2 1.6 collective-permute-start.4
  36.8 5.7 %collective-permute-done.4 = f32[128,512]{1,0:T(8,128)S(1)} collective-permute-done((f32[128,512]{1,0:T(8,128)S(1)}, f32[128,512]{1,0:T(8,128)S(1)}, u32[]{:S(2)}, u32[]{:S(2)}) %collective-permute-start.4) | collective-permute-done | bytes 262176 | tf_op jit(solution)/shard_map/cond/branch_1_fun/ppermute | solution.py:29
  42.5 0.7 add_convert_fusion
  43.2 2.1 %collective-permute-start.5 = (bf16[128,512]{1,0:T(8,128)(2,1)}, bf16[128,512]{1,0:T(8,128)(2,1)}, u32[]{:S(2)}, u32[]{:S(2)}) collective-permute-start(bf16[128,512]{1,0:T(8,128)(2,1)} %add_convert_fusion), channel_id=1, source_target_pairs={{0,1},{1,0},{2,3},{3,2},{4,5},{5,4},{6,7},{7,6},{8,9},{9,8},{10,11... | collective-permute-start | bytes 393224 | tf_op jit(solution)/shard_map/cond/branch_1_fun/ppermute | solution.py:29
  45.3 3.3 %collective-permute-done.5 = bf16[128,512]{1,0:T(8,128)(2,1)} collective-permute-done((bf16[128,512]{1,0:T(8,128)(2,1)}, bf16[128,512]{1,0:T(8,128)(2,1)}, u32[]{:S(2)}, u32[]{:S(2)}) %collective-permute-start.5) | collective-permute-done | bytes 131104 | tf_op jit(solution)/shard_map/cond/branch_1_fun/ppermute | solution.py:29
  48.5 1.6 copy-done
  50.1 1.6 copy-done.1
  51.7 1.7 tracker_half.7
  53.5 1.7 tracker_half.6
  55.3 3.0 %collective-permute-start.9 = (bf16[512,512]{1,0:T(8,128)(2,1)S(1)}, bf16[512,512]{1,0:T(8,128)(2,1)S(1)}, u32[]{:S(2)}, u32[]{:S(2)}) collective-permute-start(bf16[512,512]{1,0:T(8,128)(2,1)S(1)} %get-tuple-element.51), channel_id=1, source_target_pairs={{0,16},{2,18},{4,20},{6,22},{8,24},{10,26},{12,28},{14,30},{16,0},... | collective-permute-start | bytes 1572872 | tf_op jit(solution)/shard_map/ppermute | solution.py:34
  58.2 1.7 tracker_half.5
  60.1 1.9 tracker_half.4
  61.9 2.8 %collective-permute-start.7 = (bf16[512,512]{1,0:T(8,128)(2,1)S(1)}, bf16[512,512]{1,0:T(8,128)(2,1)S(1)}, u32[]{:S(2)}, u32[]{:S(2)}) collective-permute-start(bf16[512,512]{1,0:T(8,128)(2,1)S(1)} %get-tuple-element.47), channel_id=1, source_target_pairs={{0,16},{2,18},{4,20},{6,22},{8,24},{10,26},{12,28},{14,30},{16,0},... | collective-permute-start | bytes 1572872 | tf_op jit(solution)/shard_map/ppermute | solution.py:34
  64.8 87.7 %collective-permute-done.10.peer_half_ref = bf16[512,512]{1,0:T(8,128)(2,1)S(1)} collective-permute-done((bf16[512,512]{1,0:T(8,128)(2,1)S(1)}, bf16[512,512]{1,0:T(8,128)(2,1)S(1)}, u32[]{:S(2)}, u32[]{:S(2)}) %collective-permute-start.10) | collective-permute-done | bytes 524320 | tf_op jit(solution)/shard_map/ppermute | solution.py:34
  152.5 1.2 mix.4
  153.7 10.1 %collective-permute-done.9.peer_half_ref = bf16[512,512]{1,0:T(8,128)(2,1)S(1)} collective-permute-done((bf16[512,512]{1,0:T(8,128)(2,1)S(1)}, bf16[512,512]{1,0:T(8,128)(2,1)S(1)}, u32[]{:S(2)}, u32[]{:S(2)}) %collective-permute-start.9) | collective-permute-done | bytes 524320 | tf_op jit(solution)/shard_map/ppermute | solution.py:34
  163.8 1.1 mix.5
  164.9 10.1 %collective-permute-done.8.peer_half_ref = bf16[512,512]{1,0:T(8,128)(2,1)S(1)} collective-permute-done((bf16[512,512]{1,0:T(8,128)(2,1)S(1)}, bf16[512,512]{1,0:T(8,128)(2,1)S(1)}, u32[]{:S(2)}, u32[]{:S(2)}) %collective-permute-start.8) | collective-permute-done | bytes 524320 | tf_op jit(solution)/shard_map/ppermute | solution.py:34
  175.0 1.1 mix.6
  176.1 9.3 %collective-permute-done.7.peer_half_ref = bf16[512,512]{1,0:T(8,128)(2,1)S(1)} collective-permute-done((bf16[512,512]{1,0:T(8,128)(2,1)S(1)}, bf16[512,512]{1,0:T(8,128)(2,1)S(1)}, u32[]{:S(2)}, u32[]{:S(2)}) %collective-permute-start.7) | collective-permute-done | bytes 524320 | tf_op jit(solution)/shard_map/ppermute | solution.py:34
  185.4 1.1 mix.7
  (28 shorter events, 1.7 us)
Async XLA Ops:
  0.6 151.9 %collective-permute-start.6 = (bf16[2048,512]{1,0:T(8,128)(2,1)}, bf16[2048,512]{1,0:T(8,128)(2,1)S(1)}, u32[]{:S(2)}, u32[]{:S(2)}) collective-permute-start(bf16[2048,512]{1,0:T(8,128)(2,1)} %bitcast.25), channel_id=1, source_target_pairs={{0,16},{2,18},{4,20},{6,22},{8,24},{10,26},{12,28},{14,30},{16,0},... | collective-permute-start | bytes 6291464 | tf_op jit(solution)/shard_map/ppermute | solution.py:34
  4.7 16.3 %copy-start.3 = (bf16[2048,512]{1,0:T(8,128)(2,1)S(1)}, bf16[2048,512]{1,0:T(8,128)(2,1)}, u32[]{:S(2)}) copy-start(bf16[2048,512]{1,0:T(8,128)(2,1)} %get-tuple-element.17) | copy-start | bytes 6291460 | tf_op jit(solution)/shard_map/cond
  6.2 17.4 %copy-start.4 = (bf16[128,2048]{1,0:T(8,128)(2,1)}, bf16[128,2048]{1,0:T(8,128)(2,1)S(1)}, u32[]{:S(2)}) copy-start(bf16[128,2048]{1,0:T(8,128)(2,1)S(1)} %get-tuple-element.76) | copy-start | bytes 1572868 | tf_op jit(solution)/shard_map/cond
  6.2 14.9 %collective-permute-start = (bf16[128,2048]{1,0:T(8,128)(2,1)S(1)}, bf16[128,2048]{1,0:T(8,128)(2,1)S(1)}, u32[]{:S(2)}, u32[]{:S(2)}) collective-permute-start(bf16[128,2048]{1,0:T(8,128)(2,1)S(1)} %get-tuple-element.70), channel_id=1, source_target_pairs={{0,1},{1,0},{2,3},{3,2},{4,5},{5,4},{6,7},{7,6},{8,9},{9,8},{10,11... | collective-permute-start | bytes 1572872 | tf_op jit(solution)/shard_map/cond/branch_1_fun/ppermute | solution.py:29
  7.8 21.9 %collective-permute-start.1 = (bf16[128,512]{1,0:T(8,128)(2,1)}, bf16[128,512]{1,0:T(8,128)(2,1)S(1)}, u32[]{:S(2)}, u32[]{:S(2)}) collective-permute-start(bf16[128,512]{1,0:T(8,128)(2,1)} %bitcast.35), channel_id=1, source_target_pairs={{0,1},{1,0},{2,3},{3,2},{4,5},{5,4},{6,7},{7,6},{8,9},{9,8},{10,11... | collective-permute-start | bytes 393224 | tf_op jit(solution)/shard_map/cond/branch_1_fun/ppermute | solution.py:29
  21.0 2.5 %copy-start.6 = (bf16[128,2048]{1,0:T(8,128)(2,1)}, bf16[128,2048]{1,0:T(8,128)(2,1)S(1)}, u32[]{:S(2)}) copy-start(bf16[128,2048]{1,0:T(8,128)(2,1)S(1)} %collective-permute-done) | copy-start | bytes 1572868 | tf_op jit(solution)/shard_map/cond
  21.5 8.2 %copy-start.9 = (bf16[1,128,2048]{2,1,0:T(8,128)(2,1)S(1)}, bf16[1,128,2048]{2,1,0:T(8,128)(2,1)}, u32[]{:S(2)}) copy-start(bf16[1,128,2048]{2,1,0:T(8,128)(2,1)} %get-tuple-element.67) | copy-start | bytes 1572868 | tf_op jit(solution)/shard_map/cond
  21.5 8.2 %copy-start.10 = (bf16[1,128,512]{2,1,0:T(8,128)(2,1)S(1)}, bf16[1,128,512]{2,1,0:T(8,128)(2,1)}, u32[]{:S(2)}) copy-start(bf16[1,128,512]{2,1,0:T(8,128)(2,1)} %get-tuple-element.68) | copy-start | bytes 393220 | tf_op jit(solution)/shard_map/cond
  21.5 6.5 %collective-permute-start.2 = (f32[128,512]{1,0:T(8,128)S(1)}, f32[128,512]{1,0:T(8,128)S(1)}, u32[]{:S(2)}, u32[]{:S(2)}) collective-permute-start(f32[128,512]{1,0:T(8,128)S(1)} %fusion.1), channel_id=1, source_target_pairs={{0,1},{1,0},{2,3},{3,2},{4,5},{5,4},{6,7},{7,6},{8,9},{9,8},{10,11... | collective-permute-start | bytes 786440 | tf_op jit(solution)/shard_map/cond/branch_1_fun/ppermute | solution.py:29
  23.1 10.0 %copy-start.8 = (bf16[1,128,2048]{2,1,0:T(8,128)(2,1)S(1)}, bf16[1,128,2048]{2,1,0:T(8,128)(2,1)}, u32[]{:S(2)}) copy-start(bf16[1,128,2048]{2,1,0:T(8,128)(2,1)} %get-tuple-element.69) | copy-start | bytes 1572868 | tf_op jit(solution)/shard_map/cond
  28.1 5.0 %collective-permute-start.3 = (bf16[128,512]{1,0:T(8,128)(2,1)S(1)}, bf16[128,512]{1,0:T(8,128)(2,1)S(1)}, u32[]{:S(2)}, u32[]{:S(2)}) collective-permute-start(bf16[128,512]{1,0:T(8,128)(2,1)S(1)} %multiply_convert_fusion.refs_0_), channel_id=1, source_target_pairs={{0,1},{1,0},{2,3},{3,2},{4,5},{5,4},{6,7},{7,6},{8,9},{9,8},{10,11... | collective-permute-start | bytes 393224 | tf_op jit(solution)/shard_map/cond/branch_1_fun/ppermute | solution.py:29
  29.7 18.8 %copy-start.5 = (bf16[128,2048]{1,0:T(8,128)(2,1)S(1)}, bf16[128,2048]{1,0:T(8,128)(2,1)}, u32[]{:S(2)}) copy-start(bf16[128,2048]{1,0:T(8,128)(2,1)} %copy-done.4) | copy-start | bytes 1572868 | tf_op jit(solution)/shard_map/cond
  29.7 18.8 %copy-start.7 = (bf16[128,2048]{1,0:T(8,128)(2,1)S(1)}, bf16[128,2048]{1,0:T(8,128)(2,1)}, u32[]{:S(2)}) copy-start(bf16[128,2048]{1,0:T(8,128)(2,1)} %copy-done.6) | copy-start | bytes 1572868 | tf_op jit(solution)/shard_map/cond
  35.2 7.3 %collective-permute-start.4 = (f32[128,512]{1,0:T(8,128)S(1)}, f32[128,512]{1,0:T(8,128)S(1)}, u32[]{:S(2)}, u32[]{:S(2)}) collective-permute-start(f32[128,512]{1,0:T(8,128)S(1)} %get-tuple-element.19), channel_id=1, source_target_pairs={{0,1},{1,0},{2,3},{3,2},{4,5},{5,4},{6,7},{7,6},{8,9},{9,8},{10,11... | collective-permute-start | bytes 786440 | tf_op jit(solution)/shard_map/cond/branch_1_fun/ppermute | solution.py:29
  43.2 5.4 %collective-permute-start.5 = (bf16[128,512]{1,0:T(8,128)(2,1)}, bf16[128,512]{1,0:T(8,128)(2,1)}, u32[]{:S(2)}, u32[]{:S(2)}) collective-permute-start(bf16[128,512]{1,0:T(8,128)(2,1)} %add_convert_fusion), channel_id=1, source_target_pairs={{0,1},{1,0},{2,3},{3,2},{4,5},{5,4},{6,7},{7,6},{8,9},{9,8},{10,11... | collective-permute-start | bytes 393224 | tf_op jit(solution)/shard_map/cond/branch_1_fun/ppermute | solution.py:29
  48.5 1.6 copy-start
  50.1 1.6 copy-start.1
  53.5 99.1 %collective-permute-start.10 = (bf16[512,512]{1,0:T(8,128)(2,1)S(1)}, bf16[512,512]{1,0:T(8,128)(2,1)S(1)}, u32[]{:S(2)}, u32[]{:S(2)}) collective-permute-start(bf16[512,512]{1,0:T(8,128)(2,1)S(1)} %get-tuple-element.53), channel_id=1, source_target_pairs={{0,16},{2,18},{4,20},{6,22},{8,24},{10,26},{12,28},{14,30},{16,0},... | collective-permute-start | bytes 1572872 | tf_op jit(solution)/shard_map/ppermute | solution.py:34
  55.3 108.5 %collective-permute-start.9 = (bf16[512,512]{1,0:T(8,128)(2,1)S(1)}, bf16[512,512]{1,0:T(8,128)(2,1)S(1)}, u32[]{:S(2)}, u32[]{:S(2)}) collective-permute-start(bf16[512,512]{1,0:T(8,128)(2,1)S(1)} %get-tuple-element.51), channel_id=1, source_target_pairs={{0,16},{2,18},{4,20},{6,22},{8,24},{10,26},{12,28},{14,30},{16,0},... | collective-permute-start | bytes 1572872 | tf_op jit(solution)/shard_map/ppermute | solution.py:34
  60.0 92.5 %copy-start.2 = (bf16[1,2048,512]{2,1,0:T(8,128)(2,1)S(1)}, bf16[1,2048,512]{2,1,0:T(8,128)(2,1)}, u32[]{:S(2)}) copy-start(bf16[1,2048,512]{2,1,0:T(8,128)(2,1)} %param.13) | copy-start | bytes 6291460
  60.0 115.0 %collective-permute-start.8 = (bf16[512,512]{1,0:T(8,128)(2,1)S(1)}, bf16[512,512]{1,0:T(8,128)(2,1)S(1)}, u32[]{:S(2)}, u32[]{:S(2)}) collective-permute-start(bf16[512,512]{1,0:T(8,128)(2,1)S(1)} %get-tuple-element.49), channel_id=1, source_target_pairs={{0,16},{2,18},{4,20},{6,22},{8,24},{10,26},{12,28},{14,30},{16,0},... | collective-permute-start | bytes 1572872 | tf_op jit(solution)/shard_map/ppermute | solution.py:34
  61.9 123.4 %collective-permute-start.7 = (bf16[512,512]{1,0:T(8,128)(2,1)S(1)}, bf16[512,512]{1,0:T(8,128)(2,1)S(1)}, u32[]{:S(2)}, u32[]{:S(2)}) collective-permute-start(bf16[512,512]{1,0:T(8,128)(2,1)S(1)} %get-tuple-element.47), channel_id=1, source_target_pairs={{0,16},{2,18},{4,20},{6,22},{8,24},{10,26},{12,28},{14,30},{16,0},... | collective-permute-start | bytes 1572872 | tf_op jit(solution)/shard_map/ppermute | solution.py:34

commit v3 on v2

--- a/solution.py
+++ b/solution.py
@@ -1,4 +1,5 @@
 import functools
+import math
 
 import jax
 import jax.numpy as jnp
@@ -15,8 +16,9 @@
 
 STEP_SIZE = 0.25
 LOSS_WEIGHT = 16.0
-CHUNKS = 4
+SHARES = (5, 5, 5, 1)
 ROWS = 256
+LANES = 128
 VMEM = 32 * 1024 * 1024
 
 
@@ -116,11 +118,11 @@
     sent_ref[...] = half.astype(jnp.bfloat16)
 
 
-def tracker_chunk(chunk, rows, scale, track, old, features, cots, after):
+def tracker_chunk(start, rows, scale, track, old, features, cots):
     n, (tokens, _) = len(features), features[0].shape
     cols = track.shape[1]
-    step = min(ROWS, rows)
-    first = chunk * (rows // step)
+    step = math.gcd(start, rows, ROWS)
+    first = start // step
     moving = pl.BlockSpec((step, cols), lambda i: (first + i, 0))
     own = pl.BlockSpec((step, cols), lambda i: (i, 0))
     return pl.pallas_call(
@@ -140,26 +142,32 @@
     )(track, old, *features, *cots)
 
 
-def mix_kernel(weight_ref, peer_weight_ref, half_ref, peer_half_ref, *refs):
-    new_weight_ref, new_tracker_ref = refs[-2:]
-    both = half_ref[...] + peer_half_ref[...].astype(jnp.float32)
-    weights = weight_ref[...].astype(jnp.float32) + peer_weight_ref[...].astype(jnp.float32)
-    new_weight_ref[...] = ((weights - STEP_SIZE * both) * 0.5).astype(jnp.bfloat16)
-    new_tracker_ref[...] = (both * 0.5).astype(jnp.bfloat16)
-
-
-def mix_chunk(chunk, weight, peer_weight, half, peer_half, outs):
+def mix_kernel(start, weight_ref, peer_weight_ref, half_ref, peer_half_ref, *refs):
+    *_, new_weight_ref, new_tracker_ref, weight_out, tracker_out, sems = refs
+    copies = []
+    for slab in range(half_ref.shape[0] // LANES):
+        here = pl.ds(slab * LANES, LANES)
+        there = pl.ds(start + slab * LANES, LANES)
+        both = half_ref[here] + peer_half_ref[here].astype(jnp.float32)
+        weights = weight_ref[there].astype(jnp.float32) + peer_weight_ref[there].astype(jnp.float32)
+        weight_out[here] = ((weights - STEP_SIZE * both) * 0.5).astype(jnp.bfloat16)
+        tracker_out[here] = (both * 0.5).astype(jnp.bfloat16)
+        for i, (out, ref) in enumerate(((weight_out, new_weight_ref), (tracker_out, new_tracker_ref))):
+            copies.append(pltpu.make_async_copy(out.at[here], ref.at[there], sems.at[i, slab]))
+            copies[-1].start()
+    for copy in copies:
+        copy.wait()
+
+
+def mix_chunk(start, weight, peer_weight, half, peer_half, outs):
     rows, cols = half.shape
-    step = min(ROWS, rows)
-    first = chunk * (rows // step)
-    moving = pl.BlockSpec((step, cols), lambda i: (first + i, 0))
-    own = pl.BlockSpec((step, cols), lambda i: (i, 0))
-    return pl.pallas_call(
-        mix_kernel,
-        grid=(rows // step,),
-        in_specs=[moving, moving, own, own] + [pl.BlockSpec(memory_space=pl.ANY)] * len(outs),
-        out_specs=[moving, moving],
+    return pl.pallas_call(
+        functools.partial(mix_kernel, start),
+        in_specs=[pl.BlockSpec(memory_space=pltpu.VMEM)] * 4 + [pl.BlockSpec(memory_space=pl.ANY)] * len(outs),
+        out_specs=[pl.BlockSpec(memory_space=pl.ANY)] * 2,
         out_shape=[jax.ShapeDtypeStruct(weight.shape, jnp.bfloat16)] * 2,
+        scratch_shapes=[pltpu.VMEM((rows, cols), jnp.bfloat16)] * 2
+        + [pltpu.SemaphoreType.DMA((2, rows // LANES))],
         input_output_aliases={4 + i: i for i in range(len(outs))},
         compiler_params=params(),
         cost_estimate=pl.CostEstimate(flops=5 * rows * cols, bytes_accessed=14 * rows * cols, transcendentals=0),
@@ -197,11 +205,14 @@
 
     features, cots = lax.cond(me < n, chain, never)
 
-    rows = depth // CHUNKS
+    units = depth // LANES
+    cuts = [units * sum(SHARES[:c]) // sum(SHARES) * LANES for c in range(len(SHARES) + 1)]
     outs = ()
-    for c in range(CHUNKS):
-        half, sent = tracker_chunk(c, rows, scale, tracker[0], old_gradient[0], features, cots, None)
-        outs = mix_chunk(c, weight, peer_weight, half, partner(sent), outs)
+    for start, end in zip(cuts, cuts[1:]):
+        if start == end:
+            continue
+        half, sent = tracker_chunk(start, end - start, scale, tracker[0], old_gradient[0], features, cots)
+        outs = mix_chunk(start, weight, peer_weight, half, partner(sent), outs)
     return outs[0][None], outs[1][None]
 
 

time: 187 us -> 186 us (level)
  waiting for transfers between devices: 145 us -> 143 us
    ppermute x5, waiting for transfers between devices: 117 us -> 115 us  [partner(): return lax.ppermute(block, 'rep', [(i, i ^ 1 << ROUND) for i in range(n)])]
  transfers between devices with their start and end apart: 11 -> 11, of which waited for: 9 -> 9; matrix products, arithmetic and copies ran while one was open for 2% -> 2% of each run, Pallas kernels for 8% -> 9%
where the time goes in v3:
time: 186 us
  waiting for transfers between devices  143 us (77%)
  starting transfers between devices  19 us (10%)
  Pallas kernels  17.1 us (9%)
  local copies, waits for them, and re-layouts  4.66 us (3%)
    ppermute x5, waiting for transfers between devices, partner(): return lax.ppermute(block, 'rep', [(i, i ^ 1 << ROUND) for i in range(n)])  115 us
    ppermute x6, waiting for transfers between devices, shift(): return lax.ppermute(block, 'ctx', [(i, (i + by) % n) for i in range(n)])  27.8 us
    ppermute x5, starting transfers between devices, partner(): return lax.ppermute(block, 'rep', [(i, i ^ 1 << ROUND) for i in range(n)])  10.1 us
    ppermute x6, starting transfers between devices, shift(): return lax.ppermute(block, 'ctx', [(i, (i + by) % n) for i in range(n)])  8.95 us
    pallas_call x4, Pallas kernels, tracker_chunk(): pl.pallas_call(functools.partial(tracker_kernel, n, scale), grid=(rows //...  8.8 us
    pallas_call x4, Pallas kernels, mix_chunk(): pl.pallas_call(functools.partial(mix_kernel, start), in_specs=[pl.BlockSp...  4.4 us
  transfers between devices with their start and end apart: 11, of which 9 were waited for; matrix products, arithmetic and copies ran while one was open for 2% of the time, Pallas kernels for 9%

profile of v3, /device:TPU:0, one launch (start us, length us, event | category | flops | bytes accessed | tf_op | source)
XLA Modules:
  0.0 186.2 jit_solution(4317463092419330497)
XLA Ops:
  0.6 4.1 %collective-permute-start.6 = (bf16[2048,512]{1,0:T(8,128)(2,1)}, bf16[2048,512]{1,0:T(8,128)(2,1)S(1)}, u32[]{:S(2)}, u32[]{:S(2)}) collective-permute-start(bf16[2048,512]{1,0:T(8,128)(2,1)} %bitcast.25), channel_id=1, source_target_pairs={{0,16},{2,18},{4,20},{6,22},{8,24},{10,26},{12,28},{14,30},{16,0},... | collective-permute-start | bytes 6291464 | tf_op jit(solution)/shard_map/ppermute | solution.py:36
  4.7 43.8 %conditional.1 = (bf16[128,2048]{1,0:T(8,128)(2,1)S(1)}, bf16[128,2048]{1,0:T(8,128)(2,1)S(1)}, bf16[128,512]{1,0:T(8,128)(2,1)}, bf16[128,512]{1,0:T(8,128)(2,1)}) conditional(s32[]{:T(128)} %convert_element_type.9, () %tuple.16, (s32[]{:T(128)}, bf16[1,128,4096]{2,1,0:T(8,128)(2,1)}, bf16[1,128,2048]{2,1,0:T(8,128)(2,1)}, ...), branch_computations={%region_0.0_spmd, %region_1.2_spmd} | conditional | flops 939851776 | bytes 44827448 | solution.py:206
  4.7 1.4 dynamic-slice_bitcast_fusion
  6.2 1.6 collective-permute-start
  8.3 12.8 %collective-permute-done = bf16[128,2048]{1,0:T(8,128)(2,1)S(1)} collective-permute-done((bf16[128,2048]{1,0:T(8,128)(2,1)S(1)}, bf16[128,2048]{1,0:T(8,128)(2,1)S(1)}, u32[]{:S(2)}, u32[]{:S(2)}) %collective-permute-start) | collective-permute-done | bytes 524320 | tf_op jit(solution)/shard_map/cond/branch_1_fun/ppermute | solution.py:31
  21.5 1.6 collective-permute-start.2
  23.6 4.5 %collective-permute-done.2 = f32[128,512]{1,0:T(8,128)S(1)} collective-permute-done((f32[128,512]{1,0:T(8,128)S(1)}, f32[128,512]{1,0:T(8,128)S(1)}, u32[]{:S(2)}, u32[]{:S(2)}) %collective-permute-start.2) | collective-permute-done | bytes 262176 | tf_op jit(solution)/shard_map/cond/branch_1_fun/ppermute | solution.py:31
  28.1 1.6 collective-permute-start.3
  29.7 1.8 probabilities.1.probs_ref
  31.5 1.6 collective-permute-done.3.refs_1_
  33.1 2.1 %value_terms.1 = (f32[128,512]{1,0:T(8,128)S(1)}, f32[128,512]{1,0:T(8,128)S(1)}) custom-call(bf16[16,128,256]{2,1,0:T(8,128)(2,1)S(1)} %probabilities.1.probs_ref, bf16[128,2048]{1,0:T(8,128)(2,1)S(1)} %bitcast.33, bf16[128,512]{1,0:T(8,128)(2,1)S(1)} %multiply_convert_fusion.refs_0_, bf16[128,512]{1,0:T(8,128)(2,1)S(1)} %collective-permute-done.3.refs_1_), custom_call_target="tpu_custom_call" | custom-call | flops 268435456 | bytes 4194304 | tf_op jit(solution)/shard_map/cond/branch_1_fun/value_terms/pallas_call | solution.py:94
  35.2 1.6 collective-permute-start.4
  36.8 5.7 %collective-permute-done.4 = f32[128,512]{1,0:T(8,128)S(1)} collective-permute-done((f32[128,512]{1,0:T(8,128)S(1)}, f32[128,512]{1,0:T(8,128)S(1)}, u32[]{:S(2)}, u32[]{:S(2)}) %collective-permute-start.4) | collective-permute-done | bytes 262176 | tf_op jit(solution)/shard_map/cond/branch_1_fun/ppermute | solution.py:31
  42.5 0.7 add_convert_fusion
  43.2 2.1 %collective-permute-start.5 = (bf16[128,512]{1,0:T(8,128)(2,1)}, bf16[128,512]{1,0:T(8,128)(2,1)}, u32[]{:S(2)}, u32[]{:S(2)}) collective-permute-start(bf16[128,512]{1,0:T(8,128)(2,1)} %add_convert_fusion), channel_id=1, source_target_pairs={{0,1},{1,0},{2,3},{3,2},{4,5},{5,4},{6,7},{7,6},{8,9},{9,8},{10,11... | collective-permute-start | bytes 393224 | tf_op jit(solution)/shard_map/cond/branch_1_fun/ppermute | solution.py:31
  45.3 3.3 %collective-permute-done.5 = bf16[128,512]{1,0:T(8,128)(2,1)} collective-permute-done((bf16[128,512]{1,0:T(8,128)(2,1)}, bf16[128,512]{1,0:T(8,128)(2,1)}, u32[]{:S(2)}, u32[]{:S(2)}) %collective-permute-start.5) | collective-permute-done | bytes 131104 | tf_op jit(solution)/shard_map/cond/branch_1_fun/ppermute | solution.py:31
  48.5 1.6 copy-done
  50.1 1.6 copy-done.1
  51.7 2.5 %tracker_half.7 = (f32[640,512]{1,0:T(8,128)S(1)}, bf16[640,512]{1,0:T(8,128)(2,1)S(1)}) custom-call(bf16[2048,512]{1,0:T(8,128)(2,1)S(1)} %bitcast.17, bf16[2048,512]{1,0:T(8,128)(2,1)S(1)} %bitcast.21, bf16[128,2048]{1,0:T(8,128)(2,1)S(1)} %get-tuple-element.42.refs_0_, bf16[128,2048]{1,0:T(8,128)(2,1)S(1)} %get-tuple-element.43.refs_1_, ...), custom_call_target="tpu_custom_call" | custom-call | flops 167772160 | bytes 3276800 | tf_op jit(solution)/shard_map/tracker_half/pallas_call | solution.py:128
  54.3 2.5 %tracker_half.6 = (f32[640,512]{1,0:T(8,128)S(1)}, bf16[640,512]{1,0:T(8,128)(2,1)S(1)}) custom-call(bf16[2048,512]{1,0:T(8,128)(2,1)S(1)} %bitcast.18, bf16[2048,512]{1,0:T(8,128)(2,1)S(1)} %bitcast.22, bf16[128,2048]{1,0:T(8,128)(2,1)S(1)} %get-tuple-element.42.refs_0_, bf16[128,2048]{1,0:T(8,128)(2,1)S(1)} %get-tuple-element.43.refs_1_, ...), custom_call_target="tpu_custom_call" | custom-call | flops 167772160 | bytes 3276800 | tf_op jit(solution)/shard_map/tracker_half/pallas_call | solution.py:128
  56.8 3.0 %collective-permute-start.9 = (bf16[640,512]{1,0:T(8,128)(2,1)S(1)}, bf16[640,512]{1,0:T(8,128)(2,1)S(1)}, u32[]{:S(2)}, u32[]{:S(2)}) collective-permute-start(bf16[640,512]{1,0:T(8,128)(2,1)S(1)} %get-tuple-element.51), channel_id=1, source_target_pairs={{0,16},{2,18},{4,20},{6,22},{8,24},{10,26},{12,28},{14,30},{16,0},... | collective-permute-start | bytes 1966088 | tf_op jit(solution)/shard_map/ppermute | solution.py:36
  59.7 2.5 %tracker_half.5 = (f32[640,512]{1,0:T(8,128)S(1)}, bf16[640,512]{1,0:T(8,128)(2,1)S(1)}) custom-call(bf16[2048,512]{1,0:T(8,128)(2,1)S(1)} %bitcast.19, bf16[2048,512]{1,0:T(8,128)(2,1)S(1)} %bitcast.23, bf16[128,2048]{1,0:T(8,128)(2,1)S(1)} %get-tuple-element.42.refs_0_, bf16[128,2048]{1,0:T(8,128)(2,1)S(1)} %get-tuple-element.43.refs_1_, ...), custom_call_target="tpu_custom_call" | custom-call | flops 167772160 | bytes 3276800 | tf_op jit(solution)/shard_map/tracker_half/pallas_call | solution.py:128
  62.3 1.4 tracker_half.4
  63.7 2.8 %collective-permute-start.7 = (bf16[128,512]{1,0:T(8,128)(2,1)S(1)}, bf16[128,512]{1,0:T(8,128)(2,1)S(1)}, u32[]{:S(2)}, u32[]{:S(2)}) collective-permute-start(bf16[128,512]{1,0:T(8,128)(2,1)S(1)} %get-tuple-element.47), channel_id=1, source_target_pairs={{0,16},{2,18},{4,20},{6,22},{8,24},{10,26},{12,28},{14,30},{16,0},... | collective-permute-start | bytes 393224 | tf_op jit(solution)/shard_map/ppermute | solution.py:36
  66.5 88.8 %collective-permute-done.10.peer_half_ref = bf16[640,512]{1,0:T(8,128)(2,1)S(1)} collective-permute-done((bf16[640,512]{1,0:T(8,128)(2,1)S(1)}, bf16[640,512]{1,0:T(8,128)(2,1)S(1)}, u32[]{:S(2)}, u32[]{:S(2)}) %collective-permute-start.10) | collective-permute-done | bytes 655392 | tf_op jit(solution)/shard_map/ppermute | solution.py:36
  155.3 1.2 mix.4
  156.5 12.8 %collective-permute-done.9.peer_half_ref = bf16[640,512]{1,0:T(8,128)(2,1)S(1)} collective-permute-done((bf16[640,512]{1,0:T(8,128)(2,1)S(1)}, bf16[640,512]{1,0:T(8,128)(2,1)S(1)}, u32[]{:S(2)}, u32[]{:S(2)}) %collective-permute-start.9) | collective-permute-done | bytes 655392 | tf_op jit(solution)/shard_map/ppermute | solution.py:36
  169.4 1.2 mix.5
  170.6 12.8 %collective-permute-done.8.peer_half_ref = bf16[640,512]{1,0:T(8,128)(2,1)S(1)} collective-permute-done((bf16[640,512]{1,0:T(8,128)(2,1)S(1)}, bf16[640,512]{1,0:T(8,128)(2,1)S(1)}, u32[]{:S(2)}, u32[]{:S(2)}) %collective-permute-start.8) | collective-permute-done | bytes 655392 | tf_op jit(solution)/shard_map/ppermute | solution.py:36
  183.4 1.2 mix.6
  184.6 0.8 collective-permute-done.7.peer_half_ref
  185.4 0.8 mix.7
  (28 shorter events, 1.7 us)
Async XLA Ops:
  0.6 154.7 %collective-permute-start.6 = (bf16[2048,512]{1,0:T(8,128)(2,1)}, bf16[2048,512]{1,0:T(8,128)(2,1)S(1)}, u32[]{:S(2)}, u32[]{:S(2)}) collective-permute-start(bf16[2048,512]{1,0:T(8,128)(2,1)} %bitcast.25), channel_id=1, source_target_pairs={{0,16},{2,18},{4,20},{6,22},{8,24},{10,26},{12,28},{14,30},{16,0},... | collective-permute-start | bytes 6291464 | tf_op jit(solution)/shard_map/ppermute | solution.py:36
  4.7 16.3 %copy-start.3 = (bf16[2048,512]{1,0:T(8,128)(2,1)S(1)}, bf16[2048,512]{1,0:T(8,128)(2,1)}, u32[]{:S(2)}) copy-start(bf16[2048,512]{1,0:T(8,128)(2,1)} %get-tuple-element.17) | copy-start | bytes 6291460 | tf_op jit(solution)/shard_map/cond
  6.2 17.4 %copy-start.4 = (bf16[128,2048]{1,0:T(8,128)(2,1)}, bf16[128,2048]{1,0:T(8,128)(2,1)S(1)}, u32[]{:S(2)}) copy-start(bf16[128,2048]{1,0:T(8,128)(2,1)S(1)} %get-tuple-element.76) | copy-start | bytes 1572868 | tf_op jit(solution)/shard_map/cond
  6.2 14.9 %collective-permute-start = (bf16[128,2048]{1,0:T(8,128)(2,1)S(1)}, bf16[128,2048]{1,0:T(8,128)(2,1)S(1)}, u32[]{:S(2)}, u32[]{:S(2)}) collective-permute-start(bf16[128,2048]{1,0:T(8,128)(2,1)S(1)} %get-tuple-element.70), channel_id=1, source_target_pairs={{0,1},{1,0},{2,3},{3,2},{4,5},{5,4},{6,7},{7,6},{8,9},{9,8},{10,11... | collective-permute-start | bytes 1572872 | tf_op jit(solution)/shard_map/cond/branch_1_fun/ppermute | solution.py:31
  7.8 21.9 %collective-permute-start.1 = (bf16[128,512]{1,0:T(8,128)(2,1)}, bf16[128,512]{1,0:T(8,128)(2,1)S(1)}, u32[]{:S(2)}, u32[]{:S(2)}) collective-permute-start(bf16[128,512]{1,0:T(8,128)(2,1)} %bitcast.35), channel_id=1, source_target_pairs={{0,1},{1,0},{2,3},{3,2},{4,5},{5,4},{6,7},{7,6},{8,9},{9,8},{10,11... | collective-permute-start | bytes 393224 | tf_op jit(solution)/shard_map/cond/branch_1_fun/ppermute | solution.py:31
  21.0 2.5 %copy-start.6 = (bf16[128,2048]{1,0:T(8,128)(2,1)}, bf16[128,2048]{1,0:T(8,128)(2,1)S(1)}, u32[]{:S(2)}) copy-start(bf16[128,2048]{1,0:T(8,128)(2,1)S(1)} %collective-permute-done) | copy-start | bytes 1572868 | tf_op jit(solution)/shard_map/cond
  21.5 8.2 %copy-start.9 = (bf16[1,128,2048]{2,1,0:T(8,128)(2,1)S(1)}, bf16[1,128,2048]{2,1,0:T(8,128)(2,1)}, u32[]{:S(2)}) copy-start(bf16[1,128,2048]{2,1,0:T(8,128)(2,1)} %get-tuple-element.67) | copy-start | bytes 1572868 | tf_op jit(solution)/shard_map/cond
  21.5 8.2 %copy-start.10 = (bf16[1,128,512]{2,1,0:T(8,128)(2,1)S(1)}, bf16[1,128,512]{2,1,0:T(8,128)(2,1)}, u32[]{:S(2)}) copy-start(bf16[1,128,512]{2,1,0:T(8,128)(2,1)} %get-tuple-element.68) | copy-start | bytes 393220 | tf_op jit(solution)/shard_map/cond
  21.5 6.5 %collective-permute-start.2 = (f32[128,512]{1,0:T(8,128)S(1)}, f32[128,512]{1,0:T(8,128)S(1)}, u32[]{:S(2)}, u32[]{:S(2)}) collective-permute-start(f32[128,512]{1,0:T(8,128)S(1)} %fusion.1), channel_id=1, source_target_pairs={{0,1},{1,0},{2,3},{3,2},{4,5},{5,4},{6,7},{7,6},{8,9},{9,8},{10,11... | collective-permute-start | bytes 786440 | tf_op jit(solution)/shard_map/cond/branch_1_fun/ppermute | solution.py:31
  23.1 10.0 %copy-start.8 = (bf16[1,128,2048]{2,1,0:T(8,128)(2,1)S(1)}, bf16[1,128,2048]{2,1,0:T(8,128)(2,1)}, u32[]{:S(2)}) copy-start(bf16[1,128,2048]{2,1,0:T(8,128)(2,1)} %get-tuple-element.69) | copy-start | bytes 1572868 | tf_op jit(solution)/shard_map/cond
  28.1 5.0 %collective-permute-start.3 = (bf16[128,512]{1,0:T(8,128)(2,1)S(1)}, bf16[128,512]{1,0:T(8,128)(2,1)S(1)}, u32[]{:S(2)}, u32[]{:S(2)}) collective-permute-start(bf16[128,512]{1,0:T(8,128)(2,1)S(1)} %multiply_convert_fusion.refs_0_), channel_id=1, source_target_pairs={{0,1},{1,0},{2,3},{3,2},{4,5},{5,4},{6,7},{7,6},{8,9},{9,8},{10,11... | collective-permute-start | bytes 393224 | tf_op jit(solution)/shard_map/cond/branch_1_fun/ppermute | solution.py:31
  29.7 18.8 %copy-start.5 = (bf16[128,2048]{1,0:T(8,128)(2,1)S(1)}, bf16[128,2048]{1,0:T(8,128)(2,1)}, u32[]{:S(2)}) copy-start(bf16[128,2048]{1,0:T(8,128)(2,1)} %copy-done.4) | copy-start | bytes 1572868 | tf_op jit(solution)/shard_map/cond
  29.7 18.8 %copy-start.7 = (bf16[128,2048]{1,0:T(8,128)(2,1)S(1)}, bf16[128,2048]{1,0:T(8,128)(2,1)}, u32[]{:S(2)}) copy-start(bf16[128,2048]{1,0:T(8,128)(2,1)} %copy-done.6) | copy-start | bytes 1572868 | tf_op jit(solution)/shard_map/cond
  35.2 7.3 %collective-permute-start.4 = (f32[128,512]{1,0:T(8,128)S(1)}, f32[128,512]{1,0:T(8,128)S(1)}, u32[]{:S(2)}, u32[]{:S(2)}) collective-permute-start(f32[128,512]{1,0:T(8,128)S(1)} %get-tuple-element.19), channel_id=1, source_target_pairs={{0,1},{1,0},{2,3},{3,2},{4,5},{5,4},{6,7},{7,6},{8,9},{9,8},{10,11... | collective-permute-start | bytes 786440 | tf_op jit(solution)/shard_map/cond/branch_1_fun/ppermute | solution.py:31
  43.2 5.4 %collective-permute-start.5 = (bf16[128,512]{1,0:T(8,128)(2,1)}, bf16[128,512]{1,0:T(8,128)(2,1)}, u32[]{:S(2)}, u32[]{:S(2)}) collective-permute-start(bf16[128,512]{1,0:T(8,128)(2,1)} %add_convert_fusion), channel_id=1, source_target_pairs={{0,1},{1,0},{2,3},{3,2},{4,5},{5,4},{6,7},{7,6},{8,9},{9,8},{10,11... | collective-permute-start | bytes 393224 | tf_op jit(solution)/shard_map/cond/branch_1_fun/ppermute | solution.py:31
  48.5 1.6 copy-start
  50.1 1.6 copy-start.1
  54.2 101.1 %collective-permute-start.10 = (bf16[640,512]{1,0:T(8,128)(2,1)S(1)}, bf16[640,512]{1,0:T(8,128)(2,1)S(1)}, u32[]{:S(2)}, u32[]{:S(2)}) collective-permute-start(bf16[640,512]{1,0:T(8,128)(2,1)S(1)} %get-tuple-element.53), channel_id=1, source_target_pairs={{0,16},{2,18},{4,20},{6,22},{8,24},{10,26},{12,28},{14,30},{16,0},... | collective-permute-start | bytes 1966088 | tf_op jit(solution)/shard_map/ppermute | solution.py:36
  56.8 112.6 %collective-permute-start.9 = (bf16[640,512]{1,0:T(8,128)(2,1)S(1)}, bf16[640,512]{1,0:T(8,128)(2,1)S(1)}, u32[]{:S(2)}, u32[]{:S(2)}) collective-permute-start(bf16[640,512]{1,0:T(8,128)(2,1)S(1)} %get-tuple-element.51), channel_id=1, source_target_pairs={{0,16},{2,18},{4,20},{6,22},{8,24},{10,26},{12,28},{14,30},{16,0},... | collective-permute-start | bytes 1966088 | tf_op jit(solution)/shard_map/ppermute | solution.py:36
  62.2 93.1 %copy-start.2 = (bf16[1,2048,512]{2,1,0:T(8,128)(2,1)S(1)}, bf16[1,2048,512]{2,1,0:T(8,128)(2,1)}, u32[]{:S(2)}) copy-start(bf16[1,2048,512]{2,1,0:T(8,128)(2,1)} %param.13) | copy-start | bytes 6291460
  62.2 121.2 %collective-permute-start.8 = (bf16[640,512]{1,0:T(8,128)(2,1)S(1)}, bf16[640,512]{1,0:T(8,128)(2,1)S(1)}, u32[]{:S(2)}, u32[]{:S(2)}) collective-permute-start(bf16[640,512]{1,0:T(8,128)(2,1)S(1)} %get-tuple-element.49), channel_id=1, source_target_pairs={{0,16},{2,18},{4,20},{6,22},{8,24},{10,26},{12,28},{14,30},{16,0},... | collective-permute-start | bytes 1966088 | tf_op jit(solution)/shard_map/ppermute | solution.py:36
  63.7 121.7 %collective-permute-start.7 = (bf16[128,512]{1,0:T(8,128)(2,1)S(1)}, bf16[128,512]{1,0:T(8,128)(2,1)S(1)}, u32[]{:S(2)}, u32[]{:S(2)}) collective-permute-start(bf16[128,512]{1,0:T(8,128)(2,1)S(1)} %get-tuple-element.47), channel_id=1, source_target_pairs={{0,16},{2,18},{4,20},{6,22},{8,24},{10,26},{12,28},{14,30},{16,0},... | collective-permute-start | bytes 393224 | tf_op jit(solution)/shard_map/ppermute | solution.py:36

commit v4 on v3

--- a/solution.py
+++ b/solution.py
@@ -108,7 +108,7 @@
 
 
 def tracker_kernel(n, scale, track_ref, old_ref, *refs):
-    feature_refs, cot_refs, (wide_ref, sent_ref) = refs[:n], refs[n : 2 * n], refs[2 * n : 2 * n + 2]
+    feature_refs, cot_refs, (wide_ref, sent_ref) = refs[:n], refs[n : 2 * n], refs[-2:]
     gradient = sum(
         lax.dot_general(f[...], c[...], (((0,), (0,)), ((), ())), preferred_element_type=jnp.float32)
         for f, c in zip(feature_refs, cot_refs)
@@ -118,7 +118,7 @@
     sent_ref[...] = half.astype(jnp.bfloat16)
 
 
-def tracker_chunk(start, rows, scale, track, old, features, cots):
+def tracker_chunk(start, rows, scale, track, old, features, cots, after):
     n, (tokens, _) = len(features), features[0].shape
     cols = track.shape[1]
     step = math.gcd(start, rows, ROWS)
@@ -130,7 +130,8 @@
         grid=(rows // step,),
         in_specs=[moving, moving]
         + [pl.BlockSpec((tokens, step), lambda i: (0, first + i))] * n
-        + [pl.BlockSpec((tokens, cols), lambda i: (0, 0))] * n,
+        + [pl.BlockSpec((tokens, cols), lambda i: (0, 0))] * n
+        + [pl.BlockSpec(memory_space=pl.ANY)] * len(after),
         out_specs=[own, own],
         out_shape=[
             jax.ShapeDtypeStruct((rows, cols), jnp.float32),
@@ -139,7 +140,7 @@
         compiler_params=params(),
         cost_estimate=pl.CostEstimate(flops=2 * rows * tokens * n * cols, bytes_accessed=10 * rows * cols, transcendentals=0),
         name="tracker_half",
-    )(track, old, *features, *cots)
+    )(track, old, *features, *cots, *after)
 
 
 def mix_kernel(start, weight_ref, peer_weight_ref, half_ref, peer_half_ref, *refs):
@@ -211,7 +212,8 @@
     for start, end in zip(cuts, cuts[1:]):
         if start == end:
             continue
-        half, sent = tracker_chunk(start, end - start, scale, tracker[0], old_gradient[0], features, cots)
+        after = [peer_weight] if start else []
+        half, sent = tracker_chunk(start, end - start, scale, tracker[0], old_gradient[0], features, cots, after)
         outs = mix_chunk(start, weight, peer_weight, half, partner(sent), outs)
     return outs[0][None], outs[1][None]
 

time: 186 us -> 186 us (level)
  waiting for transfers between devices: 143 us -> 146 us
  starting transfers between devices: 19 us -> 16.4 us
    ppermute x5, waiting for transfers between devices: 115 us -> 118 us  [partner(): return lax.ppermute(block, 'rep', [(i, i ^ 1 << ROUND) for i in range(n)])]
    ppermute x5, starting transfers between devices: 10.1 us -> 7.43 us  [partner(): return lax.ppermute(block, 'rep', [(i, i ^ 1 << ROUND) for i in range(n)])]
  transfers between devices with their start and end apart: 11 -> 11, of which waited for: 9 -> 10; matrix products, arithmetic and copies ran while one was open for 2% -> 2% of each run, Pallas kernels for 9% -> 9%
where the time goes in v4:
time: 186 us
  waiting for transfers between devices  146 us (78%)
  Pallas kernels  16.9 us (9%)
  starting transfers between devices  16.4 us (9%)
  local copies, waits for them, and re-layouts  4.66 us (3%)
    ppermute x5, waiting for transfers between devices, partner(): return lax.ppermute(block, 'rep', [(i, i ^ 1 << ROUND) for i in range(n)])  118 us
    ppermute x6, waiting for transfers between devices, shift(): return lax.ppermute(block, 'ctx', [(i, (i + by) % n) for i in range(n)])  27.8 us
    ppermute x6, starting transfers between devices, shift(): return lax.ppermute(block, 'ctx', [(i, (i + by) % n) for i in range(n)])  8.95 us
    pallas_call x4, Pallas kernels, tracker_chunk(): pl.pallas_call(functools.partial(tracker_kernel, n, scale), grid=(rows //...  8.68 us
    ppermute x5, starting transfers between devices, partner(): return lax.ppermute(block, 'rep', [(i, i ^ 1 << ROUND) for i in range(n)])  7.43 us
    pallas_call x4, Pallas kernels, mix_chunk(): pl.pallas_call(functools.partial(mix_kernel, start), in_specs=[pl.BlockSp...  4.4 us
  transfers between devices with their start and end apart: 11, of which 10 were waited for; matrix products, arithmetic and copies ran while one was open for 2% of the time, Pallas kernels for 9%

profile of v4, /device:TPU:0, one launch (start us, length us, event | category | flops | bytes accessed | tf_op | source)
XLA Modules:
  0.0 186.2 jit_solution(6124181303359955042)
XLA Ops:
  0.6 4.1 %collective-permute-start.6 = (bf16[2048,512]{1,0:T(8,128)(2,1)}, bf16[2048,512]{1,0:T(8,128)(2,1)S(1)}, u32[]{:S(2)}, u32[]{:S(2)}) collective-permute-start(bf16[2048,512]{1,0:T(8,128)(2,1)} %bitcast.25), channel_id=1, source_target_pairs={{0,16},{2,18},{4,20},{6,22},{8,24},{10,26},{12,28},{14,30},{16,0},... | collective-permute-start | bytes 6291464 | tf_op jit(solution)/shard_map/ppermute | solution.py:36
  4.7 43.8 %conditional.1 = (bf16[128,2048]{1,0:T(8,128)(2,1)S(1)}, bf16[128,2048]{1,0:T(8,128)(2,1)S(1)}, bf16[128,512]{1,0:T(8,128)(2,1)}, bf16[128,512]{1,0:T(8,128)(2,1)}) conditional(s32[]{:T(128)} %convert_element_type.9, () %tuple.16, (s32[]{:T(128)}, bf16[1,128,4096]{2,1,0:T(8,128)(2,1)}, bf16[1,128,2048]{2,1,0:T(8,128)(2,1)}, ...), branch_computations={%region_0.0_spmd, %region_1.2_spmd} | conditional | flops 939851776 | bytes 44827448 | solution.py:207
  4.7 1.4 dynamic-slice_bitcast_fusion
  6.2 1.6 collective-permute-start
  8.3 12.8 %collective-permute-done = bf16[128,2048]{1,0:T(8,128)(2,1)S(1)} collective-permute-done((bf16[128,2048]{1,0:T(8,128)(2,1)S(1)}, bf16[128,2048]{1,0:T(8,128)(2,1)S(1)}, u32[]{:S(2)}, u32[]{:S(2)}) %collective-permute-start) | collective-permute-done | bytes 524320 | tf_op jit(solution)/shard_map/cond/branch_1_fun/ppermute | solution.py:31
  21.5 1.6 collective-permute-start.2
  23.6 4.5 %collective-permute-done.2 = f32[128,512]{1,0:T(8,128)S(1)} collective-permute-done((f32[128,512]{1,0:T(8,128)S(1)}, f32[128,512]{1,0:T(8,128)S(1)}, u32[]{:S(2)}, u32[]{:S(2)}) %collective-permute-start.2) | collective-permute-done | bytes 262176 | tf_op jit(solution)/shard_map/cond/branch_1_fun/ppermute | solution.py:31
  28.1 1.6 collective-permute-start.3
  29.7 1.8 probabilities.1.probs_ref
  31.5 1.6 collective-permute-done.3.refs_1_
  33.1 2.1 %value_terms.1 = (f32[128,512]{1,0:T(8,128)S(1)}, f32[128,512]{1,0:T(8,128)S(1)}) custom-call(bf16[16,128,256]{2,1,0:T(8,128)(2,1)S(1)} %probabilities.1.probs_ref, bf16[128,2048]{1,0:T(8,128)(2,1)S(1)} %bitcast.33, bf16[128,512]{1,0:T(8,128)(2,1)S(1)} %multiply_convert_fusion.refs_0_, bf16[128,512]{1,0:T(8,128)(2,1)S(1)} %collective-permute-done.3.refs_1_), custom_call_target="tpu_custom_call" | custom-call | flops 268435456 | bytes 4194304 | tf_op jit(solution)/shard_map/cond/branch_1_fun/value_terms/pallas_call | solution.py:94
  35.2 1.6 collective-permute-start.4
  36.8 5.7 %collective-permute-done.4 = f32[128,512]{1,0:T(8,128)S(1)} collective-permute-done((f32[128,512]{1,0:T(8,128)S(1)}, f32[128,512]{1,0:T(8,128)S(1)}, u32[]{:S(2)}, u32[]{:S(2)}) %collective-permute-start.4) | collective-permute-done | bytes 262176 | tf_op jit(solution)/shard_map/cond/branch_1_fun/ppermute | solution.py:31
  42.5 0.7 add_convert_fusion
  43.2 2.1 %collective-permute-start.5 = (bf16[128,512]{1,0:T(8,128)(2,1)}, bf16[128,512]{1,0:T(8,128)(2,1)}, u32[]{:S(2)}, u32[]{:S(2)}) collective-permute-start(bf16[128,512]{1,0:T(8,128)(2,1)} %add_convert_fusion), channel_id=1, source_target_pairs={{0,1},{1,0},{2,3},{3,2},{4,5},{5,4},{6,7},{7,6},{8,9},{9,8},{10,11... | collective-permute-start | bytes 393224 | tf_op jit(solution)/shard_map/cond/branch_1_fun/ppermute | solution.py:31
  45.3 3.3 %collective-permute-done.5 = bf16[128,512]{1,0:T(8,128)(2,1)} collective-permute-done((bf16[128,512]{1,0:T(8,128)(2,1)}, bf16[128,512]{1,0:T(8,128)(2,1)}, u32[]{:S(2)}, u32[]{:S(2)}) %collective-permute-start.5) | collective-permute-done | bytes 131104 | tf_op jit(solution)/shard_map/cond/branch_1_fun/ppermute | solution.py:31
  48.5 1.6 copy-done
  50.1 1.6 copy-done.1
  51.7 2.5 %tracker_half.7 = (f32[640,512]{1,0:T(8,128)S(1)}, bf16[640,512]{1,0:T(8,128)(2,1)S(1)}) custom-call(bf16[2048,512]{1,0:T(8,128)(2,1)S(1)} %bitcast.17, bf16[2048,512]{1,0:T(8,128)(2,1)S(1)} %bitcast.21, bf16[128,2048]{1,0:T(8,128)(2,1)S(1)} %get-tuple-element.42.refs_0_, bf16[128,2048]{1,0:T(8,128)(2,1)S(1)} %get-tuple-element.43.refs_1_, ...), custom_call_target="tpu_custom_call" | custom-call | flops 167772160 | bytes 3276800 | tf_op jit(solution)/shard_map/tracker_half/pallas_call | solution.py:128
  54.3 56.1 %collective-permute-done.6.refs_4_.peer_weight_ref = bf16[2048,512]{1,0:T(8,128)(2,1)S(1)} collective-permute-done((bf16[2048,512]{1,0:T(8,128)(2,1)}, bf16[2048,512]{1,0:T(8,128)(2,1)S(1)}, u32[]{:S(2)}, u32[]{:S(2)}) %collective-permute-start.6) | collective-permute-done | bytes 2097184 | tf_op jit(solution)/shard_map/ppermute | solution.py:36
  110.4 2.5 %tracker_half.6 = (f32[640,512]{1,0:T(8,128)S(1)}, bf16[640,512]{1,0:T(8,128)(2,1)S(1)}) custom-call(bf16[2048,512]{1,0:T(8,128)(2,1)S(1)} %bitcast.18, bf16[2048,512]{1,0:T(8,128)(2,1)S(1)} %bitcast.22, bf16[128,2048]{1,0:T(8,128)(2,1)S(1)} %get-tuple-element.42.refs_0_, bf16[128,2048]{1,0:T(8,128)(2,1)S(1)} %get-tuple-element.43.refs_1_, ...), custom_call_target="tpu_custom_call" | custom-call | flops 167772160 | bytes 3276800 | tf_op jit(solution)/shard_map/tracker_half/pallas_call | solution.py:128
  112.9 2.5 %tracker_half.5 = (f32[640,512]{1,0:T(8,128)S(1)}, bf16[640,512]{1,0:T(8,128)(2,1)S(1)}) custom-call(bf16[2048,512]{1,0:T(8,128)(2,1)S(1)} %bitcast.19, bf16[2048,512]{1,0:T(8,128)(2,1)S(1)} %bitcast.23, bf16[128,2048]{1,0:T(8,128)(2,1)S(1)} %get-tuple-element.42.refs_0_, bf16[128,2048]{1,0:T(8,128)(2,1)S(1)} %get-tuple-element.43.refs_1_, ...), custom_call_target="tpu_custom_call" | custom-call | flops 167772160 | bytes 3276800 | tf_op jit(solution)/shard_map/tracker_half/pallas_call | solution.py:128
  115.5 3.0 %collective-permute-start.8 = (bf16[640,512]{1,0:T(8,128)(2,1)S(1)}, bf16[640,512]{1,0:T(8,128)(2,1)S(1)}, u32[]{:S(2)}, u32[]{:S(2)}) collective-permute-start(bf16[640,512]{1,0:T(8,128)(2,1)S(1)} %get-tuple-element.49), channel_id=1, source_target_pairs={{0,16},{2,18},{4,20},{6,22},{8,24},{10,26},{12,28},{14,30},{16,0},... | collective-permute-start | bytes 1966088 | tf_op jit(solution)/shard_map/ppermute | solution.py:36
  118.4 1.2 tracker_half.4
  119.9 35.4 %collective-permute-done.10.peer_half_ref = bf16[640,512]{1,0:T(8,128)(2,1)S(1)} collective-permute-done((bf16[640,512]{1,0:T(8,128)(2,1)S(1)}, bf16[640,512]{1,0:T(8,128)(2,1)S(1)}, u32[]{:S(2)}, u32[]{:S(2)}) %collective-permute-start.10) | collective-permute-done | bytes 655392 | tf_op jit(solution)/shard_map/ppermute | solution.py:36
  155.3 1.2 mix.4
  156.5 12.8 %collective-permute-done.9.peer_half_ref = bf16[640,512]{1,0:T(8,128)(2,1)S(1)} collective-permute-done((bf16[640,512]{1,0:T(8,128)(2,1)S(1)}, bf16[640,512]{1,0:T(8,128)(2,1)S(1)}, u32[]{:S(2)}, u32[]{:S(2)}) %collective-permute-start.9) | collective-permute-done | bytes 655392 | tf_op jit(solution)/shard_map/ppermute | solution.py:36
  169.4 1.2 mix.5
  170.6 12.8 %collective-permute-done.8.peer_half_ref = bf16[640,512]{1,0:T(8,128)(2,1)S(1)} collective-permute-done((bf16[640,512]{1,0:T(8,128)(2,1)S(1)}, bf16[640,512]{1,0:T(8,128)(2,1)S(1)}, u32[]{:S(2)}, u32[]{:S(2)}) %collective-permute-start.8) | collective-permute-done | bytes 655392 | tf_op jit(solution)/shard_map/ppermute | solution.py:36
  183.4 1.2 mix.6
  184.6 0.8 collective-permute-done.7.peer_half_ref
  185.4 0.8 mix.7
  (28 shorter events, 1.9 us)
Async XLA Ops:
  0.6 109.8 %collective-permute-start.6 = (bf16[2048,512]{1,0:T(8,128)(2,1)}, bf16[2048,512]{1,0:T(8,128)(2,1)S(1)}, u32[]{:S(2)}, u32[]{:S(2)}) collective-permute-start(bf16[2048,512]{1,0:T(8,128)(2,1)} %bitcast.25), channel_id=1, source_target_pairs={{0,16},{2,18},{4,20},{6,22},{8,24},{10,26},{12,28},{14,30},{16,0},... | collective-permute-start | bytes 6291464 | tf_op jit(solution)/shard_map/ppermute | solution.py:36
  4.7 16.3 %copy-start.3 = (bf16[2048,512]{1,0:T(8,128)(2,1)S(1)}, bf16[2048,512]{1,0:T(8,128)(2,1)}, u32[]{:S(2)}) copy-start(bf16[2048,512]{1,0:T(8,128)(2,1)} %get-tuple-element.17) | copy-start | bytes 6291460 | tf_op jit(solution)/shard_map/cond
  6.2 17.4 %copy-start.4 = (bf16[128,2048]{1,0:T(8,128)(2,1)}, bf16[128,2048]{1,0:T(8,128)(2,1)S(1)}, u32[]{:S(2)}) copy-start(bf16[128,2048]{1,0:T(8,128)(2,1)S(1)} %get-tuple-element.76) | copy-start | bytes 1572868 | tf_op jit(solution)/shard_map/cond
  6.2 14.9 %collective-permute-start = (bf16[128,2048]{1,0:T(8,128)(2,1)S(1)}, bf16[128,2048]{1,0:T(8,128)(2,1)S(1)}, u32[]{:S(2)}, u32[]{:S(2)}) collective-permute-start(bf16[128,2048]{1,0:T(8,128)(2,1)S(1)} %get-tuple-element.70), channel_id=1, source_target_pairs={{0,1},{1,0},{2,3},{3,2},{4,5},{5,4},{6,7},{7,6},{8,9},{9,8},{10,11... | collective-permute-start | bytes 1572872 | tf_op jit(solution)/shard_map/cond/branch_1_fun/ppermute | solution.py:31
  7.8 21.9 %collective-permute-start.1 = (bf16[128,512]{1,0:T(8,128)(2,1)}, bf16[128,512]{1,0:T(8,128)(2,1)S(1)}, u32[]{:S(2)}, u32[]{:S(2)}) collective-permute-start(bf16[128,512]{1,0:T(8,128)(2,1)} %bitcast.35), channel_id=1, source_target_pairs={{0,1},{1,0},{2,3},{3,2},{4,5},{5,4},{6,7},{7,6},{8,9},{9,8},{10,11... | collective-permute-start | bytes 393224 | tf_op jit(solution)/shard_map/cond/branch_1_fun/ppermute | solution.py:31
  21.0 2.5 %copy-start.6 = (bf16[128,2048]{1,0:T(8,128)(2,1)}, bf16[128,2048]{1,0:T(8,128)(2,1)S(1)}, u32[]{:S(2)}) copy-start(bf16[128,2048]{1,0:T(8,128)(2,1)S(1)} %collective-permute-done) | copy-start | bytes 1572868 | tf_op jit(solution)/shard_map/cond
  21.5 8.2 %copy-start.9 = (bf16[1,128,2048]{2,1,0:T(8,128)(2,1)S(1)}, bf16[1,128,2048]{2,1,0:T(8,128)(2,1)}, u32[]{:S(2)}) copy-start(bf16[1,128,2048]{2,1,0:T(8,128)(2,1)} %get-tuple-element.67) | copy-start | bytes 1572868 | tf_op jit(solution)/shard_map/cond
  21.5 8.2 %copy-start.10 = (bf16[1,128,512]{2,1,0:T(8,128)(2,1)S(1)}, bf16[1,128,512]{2,1,0:T(8,128)(2,1)}, u32[]{:S(2)}) copy-start(bf16[1,128,512]{2,1,0:T(8,128)(2,1)} %get-tuple-element.68) | copy-start | bytes 393220 | tf_op jit(solution)/shard_map/cond
  21.5 6.5 %collective-permute-start.2 = (f32[128,512]{1,0:T(8,128)S(1)}, f32[128,512]{1,0:T(8,128)S(1)}, u32[]{:S(2)}, u32[]{:S(2)}) collective-permute-start(f32[128,512]{1,0:T(8,128)S(1)} %fusion.1), channel_id=1, source_target_pairs={{0,1},{1,0},{2,3},{3,2},{4,5},{5,4},{6,7},{7,6},{8,9},{9,8},{10,11... | collective-permute-start | bytes 786440 | tf_op jit(solution)/shard_map/cond/branch_1_fun/ppermute | solution.py:31
  23.1 10.0 %copy-start.8 = (bf16[1,128,2048]{2,1,0:T(8,128)(2,1)S(1)}, bf16[1,128,2048]{2,1,0:T(8,128)(2,1)}, u32[]{:S(2)}) copy-start(bf16[1,128,2048]{2,1,0:T(8,128)(2,1)} %get-tuple-element.69) | copy-start | bytes 1572868 | tf_op jit(solution)/shard_map/cond
  28.1 5.0 %collective-permute-start.3 = (bf16[128,512]{1,0:T(8,128)(2,1)S(1)}, bf16[128,512]{1,0:T(8,128)(2,1)S(1)}, u32[]{:S(2)}, u32[]{:S(2)}) collective-permute-start(bf16[128,512]{1,0:T(8,128)(2,1)S(1)} %multiply_convert_fusion.refs_0_), channel_id=1, source_target_pairs={{0,1},{1,0},{2,3},{3,2},{4,5},{5,4},{6,7},{7,6},{8,9},{9,8},{10,11... | collective-permute-start | bytes 393224 | tf_op jit(solution)/shard_map/cond/branch_1_fun/ppermute | solution.py:31
  29.7 18.8 %copy-start.5 = (bf16[128,2048]{1,0:T(8,128)(2,1)S(1)}, bf16[128,2048]{1,0:T(8,128)(2,1)}, u32[]{:S(2)}) copy-start(bf16[128,2048]{1,0:T(8,128)(2,1)} %copy-done.4) | copy-start | bytes 1572868 | tf_op jit(solution)/shard_map/cond
  29.7 18.8 %copy-start.7 = (bf16[128,2048]{1,0:T(8,128)(2,1)S(1)}, bf16[128,2048]{1,0:T(8,128)(2,1)}, u32[]{:S(2)}) copy-start(bf16[128,2048]{1,0:T(8,128)(2,1)} %copy-done.6) | copy-start | bytes 1572868 | tf_op jit(solution)/shard_map/cond
  35.2 7.3 %collective-permute-start.4 = (f32[128,512]{1,0:T(8,128)S(1)}, f32[128,512]{1,0:T(8,128)S(1)}, u32[]{:S(2)}, u32[]{:S(2)}) collective-permute-start(f32[128,512]{1,0:T(8,128)S(1)} %get-tuple-element.19), channel_id=1, source_target_pairs={{0,1},{1,0},{2,3},{3,2},{4,5},{5,4},{6,7},{7,6},{8,9},{9,8},{10,11... | collective-permute-start | bytes 786440 | tf_op jit(solution)/shard_map/cond/branch_1_fun/ppermute | solution.py:31
  43.2 5.4 %collective-permute-start.5 = (bf16[128,512]{1,0:T(8,128)(2,1)}, bf16[128,512]{1,0:T(8,128)(2,1)}, u32[]{:S(2)}, u32[]{:S(2)}) collective-permute-start(bf16[128,512]{1,0:T(8,128)(2,1)} %add_convert_fusion), channel_id=1, source_target_pairs={{0,1},{1,0},{2,3},{3,2},{4,5},{5,4},{6,7},{7,6},{8,9},{9,8},{10,11... | collective-permute-start | bytes 393224 | tf_op jit(solution)/shard_map/cond/branch_1_fun/ppermute | solution.py:31
  48.5 1.6 copy-start
  50.1 1.6 copy-start.1
  54.2 101.1 %collective-permute-start.10 = (bf16[640,512]{1,0:T(8,128)(2,1)S(1)}, bf16[640,512]{1,0:T(8,128)(2,1)S(1)}, u32[]{:S(2)}, u32[]{:S(2)}) collective-permute-start(bf16[640,512]{1,0:T(8,128)(2,1)S(1)} %get-tuple-element.53), channel_id=1, source_target_pairs={{0,16},{2,18},{4,20},{6,22},{8,24},{10,26},{12,28},{14,30},{16,0},... | collective-permute-start | bytes 1966088 | tf_op jit(solution)/shard_map/ppermute | solution.py:36
  112.9 56.5 %collective-permute-start.9 = (bf16[640,512]{1,0:T(8,128)(2,1)S(1)}, bf16[640,512]{1,0:T(8,128)(2,1)S(1)}, u32[]{:S(2)}, u32[]{:S(2)}) collective-permute-start(bf16[640,512]{1,0:T(8,128)(2,1)S(1)} %get-tuple-element.51), channel_id=1, source_target_pairs={{0,16},{2,18},{4,20},{6,22},{8,24},{10,26},{12,28},{14,30},{16,0},... | collective-permute-start | bytes 1966088 | tf_op jit(solution)/shard_map/ppermute | solution.py:36
  115.4 39.9 %copy-start.2 = (bf16[1,2048,512]{2,1,0:T(8,128)(2,1)S(1)}, bf16[1,2048,512]{2,1,0:T(8,128)(2,1)}, u32[]{:S(2)}) copy-start(bf16[1,2048,512]{2,1,0:T(8,128)(2,1)} %param.13) | copy-start | bytes 6291460
  115.5 68.0 %collective-permute-start.8 = (bf16[640,512]{1,0:T(8,128)(2,1)S(1)}, bf16[640,512]{1,0:T(8,128)(2,1)S(1)}, u32[]{:S(2)}, u32[]{:S(2)}) collective-permute-start(bf16[640,512]{1,0:T(8,128)(2,1)S(1)} %get-tuple-element.49), channel_id=1, source_target_pairs={{0,16},{2,18},{4,20},{6,22},{8,24},{10,26},{12,28},{14,30},{16,0},... | collective-permute-start | bytes 1966088 | tf_op jit(solution)/shard_map/ppermute | solution.py:36
  119.7 65.7 %collective-permute-start.7 = (bf16[128,512]{1,0:T(8,128)(2,1)S(1)}, bf16[128,512]{1,0:T(8,128)(2,1)S(1)}, u32[]{:S(2)}, u32[]{:S(2)}) collective-permute-start(bf16[128,512]{1,0:T(8,128)(2,1)S(1)} %get-tuple-element.47), channel_id=1, source_target_pairs={{0,16},{2,18},{4,20},{6,22},{8,24},{10,26},{12,28},{14,30},{16,0},... | collective-permute-start | bytes 393224 | tf_op jit(solution)/shard_map/ppermute | solution.py:36

commit v5 on v3

--- a/solution.py
+++ b/solution.py
@@ -108,13 +108,12 @@
 
 
 def tracker_kernel(n, scale, track_ref, old_ref, *refs):
-    feature_refs, cot_refs, (wide_ref, sent_ref) = refs[:n], refs[n : 2 * n], refs[2 * n : 2 * n + 2]
+    feature_refs, cot_refs, sent_ref = refs[:n], refs[n : 2 * n], refs[2 * n]
     gradient = sum(
         lax.dot_general(f[...], c[...], (((0,), (0,)), ((), ())), preferred_element_type=jnp.float32)
         for f, c in zip(feature_refs, cot_refs)
     )
     half = track_ref[...].astype(jnp.float32) + gradient * scale - old_ref[...].astype(jnp.float32)
-    wide_ref[...] = half
     sent_ref[...] = half.astype(jnp.bfloat16)
 
 
@@ -131,13 +130,10 @@
         in_specs=[moving, moving]
         + [pl.BlockSpec((tokens, step), lambda i: (0, first + i))] * n
         + [pl.BlockSpec((tokens, cols), lambda i: (0, 0))] * n,
-        out_specs=[own, own],
-        out_shape=[
-            jax.ShapeDtypeStruct((rows, cols), jnp.float32),
-            jax.ShapeDtypeStruct((rows, cols), jnp.bfloat16),
-        ],
-        compiler_params=params(),
-        cost_estimate=pl.CostEstimate(flops=2 * rows * tokens * n * cols, bytes_accessed=10 * rows * cols, transcendentals=0),
+        out_specs=own,
+        out_shape=jax.ShapeDtypeStruct((rows, cols), jnp.bfloat16),
+        compiler_params=params(),
+        cost_estimate=pl.CostEstimate(flops=2 * rows * tokens * n * cols, bytes_accessed=6 * rows * cols, transcendentals=0),
         name="tracker_half",
     )(track, old, *features, *cots)
 
@@ -148,7 +144,7 @@
     for slab in range(half_ref.shape[0] // LANES):
         here = pl.ds(slab * LANES, LANES)
         there = pl.ds(start + slab * LANES, LANES)
-        both = half_ref[here] + peer_half_ref[here].astype(jnp.float32)
+        both = half_ref[here].astype(jnp.float32) + peer_half_ref[here].astype(jnp.float32)
         weights = weight_ref[there].astype(jnp.float32) + peer_weight_ref[there].astype(jnp.float32)
         weight_out[here] = ((weights - STEP_SIZE * both) * 0.5).astype(jnp.bfloat16)
         tracker_out[here] = (both * 0.5).astype(jnp.bfloat16)
@@ -170,7 +166,7 @@
         + [pltpu.SemaphoreType.DMA((2, rows // LANES))],
         input_output_aliases={4 + i: i for i in range(len(outs))},
         compiler_params=params(),
-        cost_estimate=pl.CostEstimate(flops=5 * rows * cols, bytes_accessed=14 * rows * cols, transcendentals=0),
+        cost_estimate=pl.CostEstimate(flops=5 * rows * cols, bytes_accessed=12 * rows * cols, transcendentals=0),
         name="mix",
     )(weight, peer_weight, half, peer_half, *outs)
 
@@ -211,8 +207,8 @@
     for start, end in zip(cuts, cuts[1:]):
         if start == end:
             continue
-        half, sent = tracker_chunk(start, end - start, scale, tracker[0], old_gradient[0], features, cots)
-        outs = mix_chunk(start, weight, peer_weight, half, partner(sent), outs)
+        half = tracker_chunk(start, end - start, scale, tracker[0], old_gradient[0], features, cots)
+        outs = mix_chunk(start, weight, peer_weight, half, partner(half), outs)
     return outs[0][None], outs[1][None]
 
 

time: 186 us -> 189 us (1.016)
  Pallas kernels: 17.1 us -> 23.6 us
  waiting for transfers between devices: 143 us -> 138 us
    pallas_call x4, Pallas kernels: 4.4 us -> 10.9 us  [mix_chunk(): pl.pallas_call(functools.partial(mix_kernel, start), in_specs=[pl.BlockSp...]
    ppermute x5, waiting for transfers between devices: 115 us -> 110 us  [partner(): return lax.ppermute(block, 'rep', [(i, i ^ 1 << ROUND) for i in range(n)])]
  transfers between devices with their start and end apart: 11 -> 11, of which waited for: 9 -> 8; matrix products, arithmetic and copies ran while one was open for 2% -> 3% of each run, Pallas kernels for 9% -> 11%
where the time goes in v5:
time: 189 us
  waiting for transfers between devices  138 us (73%)
  Pallas kernels  23.6 us (12%)
  starting transfers between devices  20.1 us (11%)
  local copies, waits for them, and re-layouts  3.05 us (2%)
  matrix products  2.67 us (1%)
    ppermute x5, waiting for transfers between devices, partner(): return lax.ppermute(block, 'rep', [(i, i ^ 1 << ROUND) for i in range(n)])  110 us
    ppermute x6, waiting for transfers between devices, shift(): return lax.ppermute(block, 'ctx', [(i, (i + by) % n) for i in range(n)])  28 us
    pallas_call x4, Pallas kernels, mix_chunk(): pl.pallas_call(functools.partial(mix_kernel, start), in_specs=[pl.BlockSp...  10.9 us
    ppermute x5, starting transfers between devices, partner(): return lax.ppermute(block, 'rep', [(i, i ^ 1 << ROUND) for i in range(n)])  10.1 us
    ppermute x6, starting transfers between devices, shift(): return lax.ppermute(block, 'ctx', [(i, (i + by) % n) for i in range(n)])  10 us
    pallas_call x4, Pallas kernels, tracker_chunk(): pl.pallas_call(functools.partial(tracker_kernel, n, scale), grid=(rows //...  8.81 us
  transfers between devices with their start and end apart: 11, of which 8 were waited for; matrix products, arithmetic and copies ran while one was open for 3% of the time, Pallas kernels for 11%

profile of v5, /device:TPU:0, one launch (start us, length us, event | category | flops | bytes accessed | tf_op | source)
XLA Modules:
  0.0 188.7 jit_solution(708554211039708278)
XLA Ops:
  0.6 4.1 %collective-permute-start.6 = (bf16[2048,512]{1,0:T(8,128)(2,1)}, bf16[2048,512]{1,0:T(8,128)(2,1)}, u32[]{:S(2)}, u32[]{:S(2)}) collective-permute-start(bf16[2048,512]{1,0:T(8,128)(2,1)} %bitcast.25), channel_id=1, source_target_pairs={{0,16},{2,18},{4,20},{6,22},{8,24},{10,26},{12,28},{14,30},{16,0},... | collective-permute-start | bytes 6291464 | tf_op jit(solution)/shard_map/ppermute | solution.py:36
  4.7 46.8 %conditional.1 = (bf16[128,2048]{1,0:T(8,128)(2,1)S(1)}, bf16[128,2048]{1,0:T(8,128)(2,1)S(1)}, bf16[128,512]{1,0:T(8,128)(2,1)}, bf16[128,512]{1,0:T(8,128)(2,1)}) conditional(s32[]{:T(128)} %convert_element_type.9, () %tuple.16, (s32[]{:T(128)}, bf16[1,128,4096]{2,1,0:T(8,128)(2,1)}, bf16[1,128,2048]{2,1,0:T(8,128)(2,1)}, ...), branch_computations={%region_0.0_spmd, %region_1.2_spmd} | conditional | flops 939851776 | bytes 44827448 | solution.py:202
  4.7 1.4 dynamic-slice_bitcast_fusion
  6.2 1.6 collective-permute-start
  7.8 0.5 collective-permute-start.1
  8.3 12.8 %collective-permute-done = bf16[128,2048]{1,0:T(8,128)(2,1)S(1)} collective-permute-done((bf16[128,2048]{1,0:T(8,128)(2,1)S(1)}, bf16[128,2048]{1,0:T(8,128)(2,1)S(1)}, u32[]{:S(2)}, u32[]{:S(2)}) %collective-permute-start) | collective-permute-done | bytes 524320 | tf_op jit(solution)/shard_map/cond/branch_1_fun/ppermute | solution.py:31
  21.0 2.2 %fusion.1 = f32[128,512]{1,0:T(8,128)S(1)} fusion(bf16[128,2048]{1,0:T(8,128)(2,1)S(1)} %collective-permute-done, bf16[2048,512]{1,0:T(8,128)(2,1)} %get-tuple-element.17), kind=kOutput, calls=%fused_computation.5 | convolution fusion | flops 268435456 | bytes 2883584 | tf_op jit(solution)/shard_map/cond/branch_1_fun/dot_general | solution.py:188
  23.3 1.6 collective-permute-start.2
  25.3 5.0 %collective-permute-done.2 = f32[128,512]{1,0:T(8,128)S(1)} collective-permute-done((f32[128,512]{1,0:T(8,128)S(1)}, f32[128,512]{1,0:T(8,128)S(1)}, u32[]{:S(2)}, u32[]{:S(2)}) %collective-permute-start.2) | collective-permute-done | bytes 262176 | tf_op jit(solution)/shard_map/cond/branch_1_fun/ppermute | solution.py:31
  30.4 2.1 %collective-permute-start.3 = (bf16[128,512]{1,0:T(8,128)(2,1)S(1)}, bf16[128,512]{1,0:T(8,128)(2,1)S(1)}, u32[]{:S(2)}, u32[]{:S(2)}) collective-permute-start(bf16[128,512]{1,0:T(8,128)(2,1)S(1)} %multiply_convert_fusion.refs_0_), channel_id=1, source_target_pairs={{0,1},{1,0},{2,3},{3,2},{4,5},{5,4},{6,7},{7,6},{8,9},{9,8},{10,11... | collective-permute-start | bytes 393224 | tf_op jit(solution)/shard_map/cond/branch_1_fun/ppermute | solution.py:31
  32.5 1.8 probabilities.1.probs_ref
  34.3 1.2 collective-permute-done.3.refs_1_
  35.4 2.1 %value_terms.1 = (f32[128,512]{1,0:T(8,128)S(1)}, f32[128,512]{1,0:T(8,128)S(1)}) custom-call(bf16[16,128,256]{2,1,0:T(8,128)(2,1)S(1)} %probabilities.1.probs_ref, bf16[128,2048]{1,0:T(8,128)(2,1)S(1)} %bitcast.33, bf16[128,512]{1,0:T(8,128)(2,1)S(1)} %multiply_convert_fusion.refs_0_, bf16[128,512]{1,0:T(8,128)(2,1)S(1)} %collective-permute-done.3.refs_1_), custom_call_target="tpu_custom_call" | custom-call | flops 268435456 | bytes 4194304 | tf_op jit(solution)/shard_map/cond/branch_1_fun/value_terms/pallas_call | solution.py:94
  37.5 2.3 %collective-permute-start.4 = (f32[128,512]{1,0:T(8,128)S(1)}, f32[128,512]{1,0:T(8,128)S(1)}, u32[]{:S(2)}, u32[]{:S(2)}) collective-permute-start(f32[128,512]{1,0:T(8,128)S(1)} %get-tuple-element.19), channel_id=1, source_target_pairs={{0,1},{1,0},{2,3},{3,2},{4,5},{5,4},{6,7},{7,6},{8,9},{9,8},{10,11... | collective-permute-start | bytes 786440 | tf_op jit(solution)/shard_map/cond/branch_1_fun/ppermute | solution.py:31
  39.8 5.8 %collective-permute-done.4 = f32[128,512]{1,0:T(8,128)S(1)} collective-permute-done((f32[128,512]{1,0:T(8,128)S(1)}, f32[128,512]{1,0:T(8,128)S(1)}, u32[]{:S(2)}, u32[]{:S(2)}) %collective-permute-start.4) | collective-permute-done | bytes 262176 | tf_op jit(solution)/shard_map/cond/branch_1_fun/ppermute | solution.py:31
  45.5 0.7 add_convert_fusion
  46.2 2.0 %collective-permute-start.5 = (bf16[128,512]{1,0:T(8,128)(2,1)}, bf16[128,512]{1,0:T(8,128)(2,1)}, u32[]{:S(2)}, u32[]{:S(2)}) collective-permute-start(bf16[128,512]{1,0:T(8,128)(2,1)} %add_convert_fusion), channel_id=1, source_target_pairs={{0,1},{1,0},{2,3},{3,2},{4,5},{5,4},{6,7},{7,6},{8,9},{9,8},{10,11... | collective-permute-start | bytes 393224 | tf_op jit(solution)/shard_map/cond/branch_1_fun/ppermute | solution.py:31
  48.2 3.3 %collective-permute-done.5 = bf16[128,512]{1,0:T(8,128)(2,1)} collective-permute-done((bf16[128,512]{1,0:T(8,128)(2,1)}, bf16[128,512]{1,0:T(8,128)(2,1)}, u32[]{:S(2)}, u32[]{:S(2)}) %collective-permute-start.5) | collective-permute-done | bytes 131104 | tf_op jit(solution)/shard_map/cond/branch_1_fun/ppermute | solution.py:31
  51.5 1.6 copy-done.1
  53.1 2.5 %tracker_half.7.half_ref = bf16[640,512]{1,0:T(8,128)(2,1)S(1)} custom-call(bf16[2048,512]{1,0:T(8,128)(2,1)S(1)} %bitcast.17, bf16[2048,512]{1,0:T(8,128)(2,1)S(1)} %bitcast.21, bf16[128,2048]{1,0:T(8,128)(2,1)S(1)} %get-tuple-element.34.refs_0_, bf16[128,2048]{1,0:T(8,128)(2,1)S(1)} %get-tuple-element.35.refs_1_, ...), custom_call_target="tpu_custom_call" | custom-call | flops 167772160 | bytes 1966080 | tf_op jit(solution)/shard_map/tracker_half/pallas_call | solution.py:127
  55.7 2.5 %tracker_half.6.half_ref = bf16[640,512]{1,0:T(8,128)(2,1)S(1)} custom-call(bf16[2048,512]{1,0:T(8,128)(2,1)S(1)} %bitcast.18, bf16[2048,512]{1,0:T(8,128)(2,1)S(1)} %bitcast.22, bf16[128,2048]{1,0:T(8,128)(2,1)S(1)} %get-tuple-element.34.refs_0_, bf16[128,2048]{1,0:T(8,128)(2,1)S(1)} %get-tuple-element.35.refs_1_, ...), custom_call_target="tpu_custom_call" | custom-call | flops 167772160 | bytes 1966080 | tf_op jit(solution)/shard_map/tracker_half/pallas_call | solution.py:127
  58.2 3.0 %collective-permute-start.9 = (bf16[640,512]{1,0:T(8,128)(2,1)S(1)}, bf16[640,512]{1,0:T(8,128)(2,1)S(1)}, u32[]{:S(2)}, u32[]{:S(2)}) collective-permute-start(bf16[640,512]{1,0:T(8,128)(2,1)S(1)} %tracker_half.6.half_ref), channel_id=1, source_target_pairs={{0,16},{2,18},{4,20},{6,22},{8,24},{10,26},{12,28},{14,30},{16,0},... | collective-permute-start | bytes 1966088 | tf_op jit(solution)/shard_map/ppermute | solution.py:36
  61.1 2.5 %tracker_half.5.half_ref = bf16[640,512]{1,0:T(8,128)(2,1)S(1)} custom-call(bf16[2048,512]{1,0:T(8,128)(2,1)S(1)} %bitcast.19, bf16[2048,512]{1,0:T(8,128)(2,1)S(1)} %bitcast.23, bf16[128,2048]{1,0:T(8,128)(2,1)S(1)} %get-tuple-element.34.refs_0_, bf16[128,2048]{1,0:T(8,128)(2,1)S(1)} %get-tuple-element.35.refs_1_, ...), custom_call_target="tpu_custom_call" | custom-call | flops 167772160 | bytes 1966080 | tf_op jit(solution)/shard_map/tracker_half/pallas_call | solution.py:127
  63.7 1.4 tracker_half.4.half_ref
  65.1 2.8 %collective-permute-start.7 = (bf16[128,512]{1,0:T(8,128)(2,1)S(1)}, bf16[128,512]{1,0:T(8,128)(2,1)S(1)}, u32[]{:S(2)}, u32[]{:S(2)}) collective-permute-start(bf16[128,512]{1,0:T(8,128)(2,1)S(1)} %tracker_half.4.half_ref), channel_id=1, source_target_pairs={{0,16},{2,18},{4,20},{6,22},{8,24},{10,26},{12,28},{14,30},{16,0},... | collective-permute-start | bytes 393224 | tf_op jit(solution)/shard_map/ppermute | solution.py:36
  67.9 87.4 %collective-permute-done.10.peer_half_ref = bf16[640,512]{1,0:T(8,128)(2,1)S(1)} collective-permute-done((bf16[640,512]{1,0:T(8,128)(2,1)S(1)}, bf16[640,512]{1,0:T(8,128)(2,1)S(1)}, u32[]{:S(2)}, u32[]{:S(2)}) %collective-permute-start.10) | collective-permute-done | bytes 655392 | tf_op jit(solution)/shard_map/ppermute | solution.py:36
  155.3 2.8 %mix.4 = (bf16[2048,512]{1,0:T(8,128)(2,1)}, bf16[2048,512]{1,0:T(8,128)(2,1)}) custom-call(bf16[2048,512]{1,0:T(8,128)(2,1)S(1)} %bitcast.27, bf16[2048,512]{1,0:T(8,128)(2,1)} %collective-permute-done.6.peer_weight_ref, bf16[640,512]{1,0:T(8,128)(2,1)S(1)} %tracker_half.7.half_ref, bf16[640,512]{1,0:T(8,128)(2,1)S(1)} %collective-permute-done.10.peer_half_ref), custom_call_target="tpu_custom_call" | custom-call | flops 1638400 | bytes 3932160 | tf_op jit(solution)/shard_map/mix/pallas_call | solution.py:160
  158.2 11.2 %collective-permute-done.9.peer_half_ref = bf16[640,512]{1,0:T(8,128)(2,1)S(1)} collective-permute-done((bf16[640,512]{1,0:T(8,128)(2,1)S(1)}, bf16[640,512]{1,0:T(8,128)(2,1)S(1)}, u32[]{:S(2)}, u32[]{:S(2)}) %collective-permute-start.9) | collective-permute-done | bytes 655392 | tf_op jit(solution)/shard_map/ppermute | solution.py:36
  169.4 2.8 %mix.5 = (bf16[2048,512]{1,0:T(8,128)(2,1)}, bf16[2048,512]{1,0:T(8,128)(2,1)}) custom-call(bf16[2048,512]{1,0:T(8,128)(2,1)S(1)} %bitcast.28, bf16[2048,512]{1,0:T(8,128)(2,1)} %collective-permute-done.6.peer_weight_ref, bf16[640,512]{1,0:T(8,128)(2,1)S(1)} %tracker_half.6.half_ref, ...), custom_call_target="tpu_custom_call", output_to_operand_aliasing={{0}: (4, {}), {1}: (5, {})} | custom-call | flops 1638400 | bytes 3932160 | tf_op jit(solution)/shard_map/mix/pallas_call | solution.py:160
  172.2 11.2 %collective-permute-done.8.peer_half_ref = bf16[640,512]{1,0:T(8,128)(2,1)S(1)} collective-permute-done((bf16[640,512]{1,0:T(8,128)(2,1)S(1)}, bf16[640,512]{1,0:T(8,128)(2,1)S(1)}, u32[]{:S(2)}, u32[]{:S(2)}) %collective-permute-start.8) | collective-permute-done | bytes 655392 | tf_op jit(solution)/shard_map/ppermute | solution.py:36
  183.4 2.8 %mix.6 = (bf16[2048,512]{1,0:T(8,128)(2,1)}, bf16[2048,512]{1,0:T(8,128)(2,1)}) custom-call(bf16[2048,512]{1,0:T(8,128)(2,1)S(1)} %bitcast.29, bf16[2048,512]{1,0:T(8,128)(2,1)} %collective-permute-done.6.peer_weight_ref, bf16[640,512]{1,0:T(8,128)(2,1)S(1)} %tracker_half.5.half_ref, ...), custom_call_target="tpu_custom_call", output_to_operand_aliasing={{0}: (4, {}), {1}: (5, {})} | custom-call | flops 1638400 | bytes 3932160 | tf_op jit(solution)/shard_map/mix/pallas_call | solution.py:160
  186.3 2.4 %mix.7 = (bf16[2048,512]{1,0:T(8,128)(2,1)}, bf16[2048,512]{1,0:T(8,128)(2,1)}) custom-call(bf16[2048,512]{1,0:T(8,128)(2,1)S(1)} %bitcast.30, bf16[2048,512]{1,0:T(8,128)(2,1)} %collective-permute-done.6.peer_weight_ref, bf16[128,512]{1,0:T(8,128)(2,1)S(1)} %tracker_half.4.half_ref, ...), custom_call_target="tpu_custom_call", output_to_operand_aliasing={{0}: (4, {}), {1}: (5, {})} | custom-call | flops 327680 | bytes 786432 | tf_op jit(solution)/shard_map/mix/pallas_call | solution.py:160
  (28 shorter events, 0.7 us)
Async XLA Ops:
  0.6 154.7 %collective-permute-start.6 = (bf16[2048,512]{1,0:T(8,128)(2,1)}, bf16[2048,512]{1,0:T(8,128)(2,1)}, u32[]{:S(2)}, u32[]{:S(2)}) collective-permute-start(bf16[2048,512]{1,0:T(8,128)(2,1)} %bitcast.25), channel_id=1, source_target_pairs={{0,16},{2,18},{4,20},{6,22},{8,24},{10,26},{12,28},{14,30},{16,0},... | collective-permute-start | bytes 6291464 | tf_op jit(solution)/shard_map/ppermute | solution.py:36
  4.7 46.8 %copy-start = (bf16[1,2048,512]{2,1,0:T(8,128)(2,1)S(1)}, bf16[1,2048,512]{2,1,0:T(8,128)(2,1)}, u32[]{:S(2)}) copy-start(bf16[1,2048,512]{2,1,0:T(8,128)(2,1)} %param.14) | copy-start | bytes 6291460
  4.7 3.0 %copy-start.10 = (bf16[1,128,512]{2,1,0:T(8,128)(2,1)S(1)}, bf16[1,128,512]{2,1,0:T(8,128)(2,1)}, u32[]{:S(2)}) copy-start(bf16[1,128,512]{2,1,0:T(8,128)(2,1)} %get-tuple-element.52) | copy-start | bytes 393220 | tf_op jit(solution)/shard_map/cond
  4.7 20.1 %copy-start.3 = (bf16[2048,512]{1,0:T(8,128)(2,1)S(1)}, bf16[2048,512]{1,0:T(8,128)(2,1)}, u32[]{:S(2)}) copy-start(bf16[2048,512]{1,0:T(8,128)(2,1)} %get-tuple-element.17) | copy-start | bytes 6291460 | tf_op jit(solution)/shard_map/cond
  6.2 19.2 %copy-start.4 = (bf16[128,2048]{1,0:T(8,128)(2,1)}, bf16[128,2048]{1,0:T(8,128)(2,1)S(1)}, u32[]{:S(2)}) copy-start(bf16[128,2048]{1,0:T(8,128)(2,1)S(1)} %get-tuple-element.60) | copy-start | bytes 1572868 | tf_op jit(solution)/shard_map/cond
  6.2 14.9 %collective-permute-start = (bf16[128,2048]{1,0:T(8,128)(2,1)S(1)}, bf16[128,2048]{1,0:T(8,128)(2,1)S(1)}, u32[]{:S(2)}, u32[]{:S(2)}) collective-permute-start(bf16[128,2048]{1,0:T(8,128)(2,1)S(1)} %get-tuple-element.54), channel_id=1, source_target_pairs={{0,1},{1,0},{2,3},{3,2},{4,5},{5,4},{6,7},{7,6},{8,9},{9,8},{10,11... | collective-permute-start | bytes 1572872 | tf_op jit(solution)/shard_map/cond/branch_1_fun/ppermute | solution.py:31
  7.8 24.7 %collective-permute-start.1 = (bf16[128,512]{1,0:T(8,128)(2,1)S(1)}, bf16[128,512]{1,0:T(8,128)(2,1)S(1)}, u32[]{:S(2)}, u32[]{:S(2)}) collective-permute-start(bf16[128,512]{1,0:T(8,128)(2,1)S(1)} %bitcast.35), channel_id=1, source_target_pairs={{0,1},{1,0},{2,3},{3,2},{4,5},{5,4},{6,7},{7,6},{8,9},{9,8},{10,11... | collective-permute-start | bytes 393224 | tf_op jit(solution)/shard_map/cond/branch_1_fun/ppermute | solution.py:31
  21.0 4.3 %copy-start.6 = (bf16[128,2048]{1,0:T(8,128)(2,1)}, bf16[128,2048]{1,0:T(8,128)(2,1)S(1)}, u32[]{:S(2)}) copy-start(bf16[128,2048]{1,0:T(8,128)(2,1)S(1)} %collective-permute-done) | copy-start | bytes 1572868 | tf_op jit(solution)/shard_map/cond
  23.3 9.2 %copy-start.9 = (bf16[1,128,2048]{2,1,0:T(8,128)(2,1)S(1)}, bf16[1,128,2048]{2,1,0:T(8,128)(2,1)}, u32[]{:S(2)}) copy-start(bf16[1,128,2048]{2,1,0:T(8,128)(2,1)} %get-tuple-element.51) | copy-start | bytes 1572868 | tf_op jit(solution)/shard_map/cond
  23.3 7.1 %collective-permute-start.2 = (f32[128,512]{1,0:T(8,128)S(1)}, f32[128,512]{1,0:T(8,128)S(1)}, u32[]{:S(2)}, u32[]{:S(2)}) collective-permute-start(f32[128,512]{1,0:T(8,128)S(1)} %fusion.1), channel_id=1, source_target_pairs={{0,1},{1,0},{2,3},{3,2},{4,5},{5,4},{6,7},{7,6},{8,9},{9,8},{10,11... | collective-permute-start | bytes 786440 | tf_op jit(solution)/shard_map/cond/branch_1_fun/ppermute | solution.py:31
  24.9 10.6 %copy-start.8 = (bf16[1,128,2048]{2,1,0:T(8,128)(2,1)S(1)}, bf16[1,128,2048]{2,1,0:T(8,128)(2,1)}, u32[]{:S(2)}) copy-start(bf16[1,128,2048]{2,1,0:T(8,128)(2,1)} %get-tuple-element.53) | copy-start | bytes 1572868 | tf_op jit(solution)/shard_map/cond
  30.4 5.0 %collective-permute-start.3 = (bf16[128,512]{1,0:T(8,128)(2,1)S(1)}, bf16[128,512]{1,0:T(8,128)(2,1)S(1)}, u32[]{:S(2)}, u32[]{:S(2)}) collective-permute-start(bf16[128,512]{1,0:T(8,128)(2,1)S(1)} %multiply_convert_fusion.refs_0_), channel_id=1, source_target_pairs={{0,1},{1,0},{2,3},{3,2},{4,5},{5,4},{6,7},{7,6},{8,9},{9,8},{10,11... | collective-permute-start | bytes 393224 | tf_op jit(solution)/shard_map/cond/branch_1_fun/ppermute | solution.py:31
  32.5 19.0 %copy-start.5 = (bf16[128,2048]{1,0:T(8,128)(2,1)S(1)}, bf16[128,2048]{1,0:T(8,128)(2,1)}, u32[]{:S(2)}) copy-start(bf16[128,2048]{1,0:T(8,128)(2,1)} %copy-done.4) | copy-start | bytes 1572868 | tf_op jit(solution)/shard_map/cond
  32.5 19.0 %copy-start.7 = (bf16[128,2048]{1,0:T(8,128)(2,1)S(1)}, bf16[128,2048]{1,0:T(8,128)(2,1)}, u32[]{:S(2)}) copy-start(bf16[128,2048]{1,0:T(8,128)(2,1)} %copy-done.6) | copy-start | bytes 1572868 | tf_op jit(solution)/shard_map/cond
  37.5 8.0 %collective-permute-start.4 = (f32[128,512]{1,0:T(8,128)S(1)}, f32[128,512]{1,0:T(8,128)S(1)}, u32[]{:S(2)}, u32[]{:S(2)}) collective-permute-start(f32[128,512]{1,0:T(8,128)S(1)} %get-tuple-element.19), channel_id=1, source_target_pairs={{0,1},{1,0},{2,3},{3,2},{4,5},{5,4},{6,7},{7,6},{8,9},{9,8},{10,11... | collective-permute-start | bytes 786440 | tf_op jit(solution)/shard_map/cond/branch_1_fun/ppermute | solution.py:31
  46.2 5.3 %collective-permute-start.5 = (bf16[128,512]{1,0:T(8,128)(2,1)}, bf16[128,512]{1,0:T(8,128)(2,1)}, u32[]{:S(2)}, u32[]{:S(2)}) collective-permute-start(bf16[128,512]{1,0:T(8,128)(2,1)} %add_convert_fusion), channel_id=1, source_target_pairs={{0,1},{1,0},{2,3},{3,2},{4,5},{5,4},{6,7},{7,6},{8,9},{9,8},{10,11... | collective-permute-start | bytes 393224 | tf_op jit(solution)/shard_map/cond/branch_1_fun/ppermute | solution.py:31
  51.5 1.6 copy-start.1
  55.6 99.8 %collective-permute-start.10 = (bf16[640,512]{1,0:T(8,128)(2,1)S(1)}, bf16[640,512]{1,0:T(8,128)(2,1)S(1)}, u32[]{:S(2)}, u32[]{:S(2)}) collective-permute-start(bf16[640,512]{1,0:T(8,128)(2,1)S(1)} %tracker_half.7.half_ref), channel_id=1, source_target_pairs={{0,16},{2,18},{4,20},{6,22},{8,24},{10,26},{12,28},{14,30},{16,0},... | collective-permute-start | bytes 1966088 | tf_op jit(solution)/shard_map/ppermute | solution.py:36
  58.2 111.2 %collective-permute-start.9 = (bf16[640,512]{1,0:T(8,128)(2,1)S(1)}, bf16[640,512]{1,0:T(8,128)(2,1)S(1)}, u32[]{:S(2)}, u32[]{:S(2)}) collective-permute-start(bf16[640,512]{1,0:T(8,128)(2,1)S(1)} %tracker_half.6.half_ref), channel_id=1, source_target_pairs={{0,16},{2,18},{4,20},{6,22},{8,24},{10,26},{12,28},{14,30},{16,0},... | collective-permute-start | bytes 1966088 | tf_op jit(solution)/shard_map/ppermute | solution.py:36
  63.6 91.7 %copy-start.2 = (bf16[1,2048,512]{2,1,0:T(8,128)(2,1)S(1)}, bf16[1,2048,512]{2,1,0:T(8,128)(2,1)}, u32[]{:S(2)}) copy-start(bf16[1,2048,512]{2,1,0:T(8,128)(2,1)} %param.13) | copy-start | bytes 6291460
  63.6 119.8 %collective-permute-start.8 = (bf16[640,512]{1,0:T(8,128)(2,1)S(1)}, bf16[640,512]{1,0:T(8,128)(2,1)S(1)}, u32[]{:S(2)}, u32[]{:S(2)}) collective-permute-start(bf16[640,512]{1,0:T(8,128)(2,1)S(1)} %tracker_half.5.half_ref), channel_id=1, source_target_pairs={{0,16},{2,18},{4,20},{6,22},{8,24},{10,26},{12,28},{14,30},{16,0},... | collective-permute-start | bytes 1966088 | tf_op jit(solution)/shard_map/ppermute | solution.py:36
  65.1 121.2 %collective-permute-start.7 = (bf16[128,512]{1,0:T(8,128)(2,1)S(1)}, bf16[128,512]{1,0:T(8,128)(2,1)S(1)}, u32[]{:S(2)}, u32[]{:S(2)}) collective-permute-start(bf16[128,512]{1,0:T(8,128)(2,1)S(1)} %tracker_half.4.half_ref), channel_id=1, source_target_pairs={{0,16},{2,18},{4,20},{6,22},{8,24},{10,26},{12,28},{14,30},{16,0},... | collective-permute-start | bytes 393224 | tf_op jit(solution)/shard_map/ppermute | solution.py:36

commit v6 on v3

--- a/solution.py
+++ b/solution.py
@@ -19,6 +19,7 @@
 SHARES = (5, 5, 5, 1)
 ROWS = 256
 LANES = 128
+SLAB = 64
 VMEM = 32 * 1024 * 1024
 
 
@@ -145,9 +146,9 @@
 def mix_kernel(start, weight_ref, peer_weight_ref, half_ref, peer_half_ref, *refs):
     *_, new_weight_ref, new_tracker_ref, weight_out, tracker_out, sems = refs
     copies = []
-    for slab in range(half_ref.shape[0] // LANES):
-        here = pl.ds(slab * LANES, LANES)
-        there = pl.ds(start + slab * LANES, LANES)
+    for slab in range(half_ref.shape[0] // SLAB):
+        here = pl.ds(slab * SLAB, SLAB)
+        there = pl.ds(start + slab * SLAB, SLAB)
         both = half_ref[here] + peer_half_ref[here].astype(jnp.float32)
         weights = weight_ref[there].astype(jnp.float32) + peer_weight_ref[there].astype(jnp.float32)
         weight_out[here] = ((weights - STEP_SIZE * both) * 0.5).astype(jnp.bfloat16)
@@ -167,7 +168,7 @@
         out_specs=[pl.BlockSpec(memory_space=pl.ANY)] * 2,
         out_shape=[jax.ShapeDtypeStruct(weight.shape, jnp.bfloat16)] * 2,
         scratch_shapes=[pltpu.VMEM((rows, cols), jnp.bfloat16)] * 2
-        + [pltpu.SemaphoreType.DMA((2, rows // LANES))],
+        + [pltpu.SemaphoreType.DMA((2, rows // SLAB))],
         input_output_aliases={4 + i: i for i in range(len(outs))},
         compiler_params=params(),
         cost_estimate=pl.CostEstimate(flops=5 * rows * cols, bytes_accessed=14 * rows * cols, transcendentals=0),

time: 186 us -> 186 us (level)
  no operation moved by 1% of the time
where the time goes in v6:
time: 186 us
  waiting for transfers between devices  143 us (77%)
  starting transfers between devices  19 us (10%)
  Pallas kernels  17.2 us (9%)
  local copies, waits for them, and re-layouts  4.66 us (3%)
    ppermute x5, waiting for transfers between devices, partner(): return lax.ppermute(block, 'rep', [(i, i ^ 1 << ROUND) for i in range(n)])  115 us
    ppermute x6, waiting for transfers between devices, shift(): return lax.ppermute(block, 'ctx', [(i, (i + by) % n) for i in range(n)])  27.8 us
    ppermute x5, starting transfers between devices, partner(): return lax.ppermute(block, 'rep', [(i, i ^ 1 << ROUND) for i in range(n)])  10.1 us
    ppermute x6, starting transfers between devices, shift(): return lax.ppermute(block, 'ctx', [(i, (i + by) % n) for i in range(n)])  8.95 us
    pallas_call x4, Pallas kernels, tracker_chunk(): pl.pallas_call(functools.partial(tracker_kernel, n, scale), grid=(rows //...  8.8 us
    pallas_call x4, Pallas kernels, mix_chunk(): pl.pallas_call(functools.partial(mix_kernel, start), in_specs=[pl.BlockSp...  4.51 us
  transfers between devices with their start and end apart: 11, of which 9 were waited for; matrix products, arithmetic and copies ran while one was open for 2% of the time, Pallas kernels for 9%

profile of v6, /device:TPU:0, one launch (start us, length us, event | category | flops | bytes accessed | tf_op | source)
XLA Modules:
  0.0 186.2 jit_solution(2345050856506075363)
XLA Ops:
  0.6 4.1 %collective-permute-start.6 = (bf16[2048,512]{1,0:T(8,128)(2,1)}, bf16[2048,512]{1,0:T(8,128)(2,1)S(1)}, u32[]{:S(2)}, u32[]{:S(2)}) collective-permute-start(bf16[2048,512]{1,0:T(8,128)(2,1)} %bitcast.25), channel_id=1, source_target_pairs={{0,16},{2,18},{4,20},{6,22},{8,24},{10,26},{12,28},{14,30},{16,0},... | collective-permute-start | bytes 6291464 | tf_op jit(solution)/shard_map/ppermute | solution.py:37
  4.7 43.8 %conditional.1 = (bf16[128,2048]{1,0:T(8,128)(2,1)S(1)}, bf16[128,2048]{1,0:T(8,128)(2,1)S(1)}, bf16[128,512]{1,0:T(8,128)(2,1)}, bf16[128,512]{1,0:T(8,128)(2,1)}) conditional(s32[]{:T(128)} %convert_element_type.9, () %tuple.16, (s32[]{:T(128)}, bf16[1,128,4096]{2,1,0:T(8,128)(2,1)}, bf16[1,128,2048]{2,1,0:T(8,128)(2,1)}, ...), branch_computations={%region_0.0_spmd, %region_1.2_spmd} | conditional | flops 939851776 | bytes 44827448 | solution.py:207
  4.7 1.4 dynamic-slice_bitcast_fusion
  6.2 1.6 collective-permute-start
  8.3 12.8 %collective-permute-done = bf16[128,2048]{1,0:T(8,128)(2,1)S(1)} collective-permute-done((bf16[128,2048]{1,0:T(8,128)(2,1)S(1)}, bf16[128,2048]{1,0:T(8,128)(2,1)S(1)}, u32[]{:S(2)}, u32[]{:S(2)}) %collective-permute-start) | collective-permute-done | bytes 524320 | tf_op jit(solution)/shard_map/cond/branch_1_fun/ppermute | solution.py:32
  21.5 1.6 collective-permute-start.2
  23.6 4.5 %collective-permute-done.2 = f32[128,512]{1,0:T(8,128)S(1)} collective-permute-done((f32[128,512]{1,0:T(8,128)S(1)}, f32[128,512]{1,0:T(8,128)S(1)}, u32[]{:S(2)}, u32[]{:S(2)}) %collective-permute-start.2) | collective-permute-done | bytes 262176 | tf_op jit(solution)/shard_map/cond/branch_1_fun/ppermute | solution.py:32
  28.1 1.6 collective-permute-start.3
  29.7 1.8 probabilities.1.probs_ref
  31.5 1.6 collective-permute-done.3.refs_1_
  33.1 2.1 %value_terms.1 = (f32[128,512]{1,0:T(8,128)S(1)}, f32[128,512]{1,0:T(8,128)S(1)}) custom-call(bf16[16,128,256]{2,1,0:T(8,128)(2,1)S(1)} %probabilities.1.probs_ref, bf16[128,2048]{1,0:T(8,128)(2,1)S(1)} %bitcast.33, bf16[128,512]{1,0:T(8,128)(2,1)S(1)} %multiply_convert_fusion.refs_0_, bf16[128,512]{1,0:T(8,128)(2,1)S(1)} %collective-permute-done.3.refs_1_), custom_call_target="tpu_custom_call" | custom-call | flops 268435456 | bytes 4194304 | tf_op jit(solution)/shard_map/cond/branch_1_fun/value_terms/pallas_call | solution.py:95
  35.2 1.6 collective-permute-start.4
  36.8 5.7 %collective-permute-done.4 = f32[128,512]{1,0:T(8,128)S(1)} collective-permute-done((f32[128,512]{1,0:T(8,128)S(1)}, f32[128,512]{1,0:T(8,128)S(1)}, u32[]{:S(2)}, u32[]{:S(2)}) %collective-permute-start.4) | collective-permute-done | bytes 262176 | tf_op jit(solution)/shard_map/cond/branch_1_fun/ppermute | solution.py:32
  42.5 0.7 add_convert_fusion
  43.2 2.1 %collective-permute-start.5 = (bf16[128,512]{1,0:T(8,128)(2,1)}, bf16[128,512]{1,0:T(8,128)(2,1)}, u32[]{:S(2)}, u32[]{:S(2)}) collective-permute-start(bf16[128,512]{1,0:T(8,128)(2,1)} %add_convert_fusion), channel_id=1, source_target_pairs={{0,1},{1,0},{2,3},{3,2},{4,5},{5,4},{6,7},{7,6},{8,9},{9,8},{10,11... | collective-permute-start | bytes 393224 | tf_op jit(solution)/shard_map/cond/branch_1_fun/ppermute | solution.py:32
  45.3 3.3 %collective-permute-done.5 = bf16[128,512]{1,0:T(8,128)(2,1)} collective-permute-done((bf16[128,512]{1,0:T(8,128)(2,1)}, bf16[128,512]{1,0:T(8,128)(2,1)}, u32[]{:S(2)}, u32[]{:S(2)}) %collective-permute-start.5) | collective-permute-done | bytes 131104 | tf_op jit(solution)/shard_map/cond/branch_1_fun/ppermute | solution.py:32
  48.5 1.6 copy-done
  50.1 1.6 copy-done.1
  51.7 2.5 %tracker_half.7 = (f32[640,512]{1,0:T(8,128)S(1)}, bf16[640,512]{1,0:T(8,128)(2,1)S(1)}) custom-call(bf16[2048,512]{1,0:T(8,128)(2,1)S(1)} %bitcast.17, bf16[2048,512]{1,0:T(8,128)(2,1)S(1)} %bitcast.21, bf16[128,2048]{1,0:T(8,128)(2,1)S(1)} %get-tuple-element.42.refs_0_, bf16[128,2048]{1,0:T(8,128)(2,1)S(1)} %get-tuple-element.43.refs_1_, ...), custom_call_target="tpu_custom_call" | custom-call | flops 167772160 | bytes 3276800 | tf_op jit(solution)/shard_map/tracker_half/pallas_call | solution.py:129
  54.3 2.5 %tracker_half.6 = (f32[640,512]{1,0:T(8,128)S(1)}, bf16[640,512]{1,0:T(8,128)(2,1)S(1)}) custom-call(bf16[2048,512]{1,0:T(8,128)(2,1)S(1)} %bitcast.18, bf16[2048,512]{1,0:T(8,128)(2,1)S(1)} %bitcast.22, bf16[128,2048]{1,0:T(8,128)(2,1)S(1)} %get-tuple-element.42.refs_0_, bf16[128,2048]{1,0:T(8,128)(2,1)S(1)} %get-tuple-element.43.refs_1_, ...), custom_call_target="tpu_custom_call" | custom-call | flops 167772160 | bytes 3276800 | tf_op jit(solution)/shard_map/tracker_half/pallas_call | solution.py:129
  56.8 3.0 %collective-permute-start.9 = (bf16[640,512]{1,0:T(8,128)(2,1)S(1)}, bf16[640,512]{1,0:T(8,128)(2,1)S(1)}, u32[]{:S(2)}, u32[]{:S(2)}) collective-permute-start(bf16[640,512]{1,0:T(8,128)(2,1)S(1)} %get-tuple-element.51), channel_id=1, source_target_pairs={{0,16},{2,18},{4,20},{6,22},{8,24},{10,26},{12,28},{14,30},{16,0},... | collective-permute-start | bytes 1966088 | tf_op jit(solution)/shard_map/ppermute | solution.py:37
  59.7 2.5 %tracker_half.5 = (f32[640,512]{1,0:T(8,128)S(1)}, bf16[640,512]{1,0:T(8,128)(2,1)S(1)}) custom-call(bf16[2048,512]{1,0:T(8,128)(2,1)S(1)} %bitcast.19, bf16[2048,512]{1,0:T(8,128)(2,1)S(1)} %bitcast.23, bf16[128,2048]{1,0:T(8,128)(2,1)S(1)} %get-tuple-element.42.refs_0_, bf16[128,2048]{1,0:T(8,128)(2,1)S(1)} %get-tuple-element.43.refs_1_, ...), custom_call_target="tpu_custom_call" | custom-call | flops 167772160 | bytes 3276800 | tf_op jit(solution)/shard_map/tracker_half/pallas_call | solution.py:129
  62.3 1.4 tracker_half.4
  63.7 2.8 %collective-permute-start.7 = (bf16[128,512]{1,0:T(8,128)(2,1)S(1)}, bf16[128,512]{1,0:T(8,128)(2,1)S(1)}, u32[]{:S(2)}, u32[]{:S(2)}) collective-permute-start(bf16[128,512]{1,0:T(8,128)(2,1)S(1)} %get-tuple-element.47), channel_id=1, source_target_pairs={{0,16},{2,18},{4,20},{6,22},{8,24},{10,26},{12,28},{14,30},{16,0},... | collective-permute-start | bytes 393224 | tf_op jit(solution)/shard_map/ppermute | solution.py:37
  66.5 88.8 %collective-permute-done.10.peer_half_ref = bf16[640,512]{1,0:T(8,128)(2,1)S(1)} collective-permute-done((bf16[640,512]{1,0:T(8,128)(2,1)S(1)}, bf16[640,512]{1,0:T(8,128)(2,1)S(1)}, u32[]{:S(2)}, u32[]{:S(2)}) %collective-permute-start.10) | collective-permute-done | bytes 655392 | tf_op jit(solution)/shard_map/ppermute | solution.py:37
  155.3 1.2 mix.4
  156.6 12.8 %collective-permute-done.9.peer_half_ref = bf16[640,512]{1,0:T(8,128)(2,1)S(1)} collective-permute-done((bf16[640,512]{1,0:T(8,128)(2,1)S(1)}, bf16[640,512]{1,0:T(8,128)(2,1)S(1)}, u32[]{:S(2)}, u32[]{:S(2)}) %collective-permute-start.9) | collective-permute-done | bytes 655392 | tf_op jit(solution)/shard_map/ppermute | solution.py:37
  169.4 1.2 mix.5
  170.6 12.8 %collective-permute-done.8.peer_half_ref = bf16[640,512]{1,0:T(8,128)(2,1)S(1)} collective-permute-done((bf16[640,512]{1,0:T(8,128)(2,1)S(1)}, bf16[640,512]{1,0:T(8,128)(2,1)S(1)}, u32[]{:S(2)}, u32[]{:S(2)}) %collective-permute-start.8) | collective-permute-done | bytes 655392 | tf_op jit(solution)/shard_map/ppermute | solution.py:37
  183.4 1.2 mix.6
  184.7 0.7 collective-permute-done.7.peer_half_ref
  185.4 0.8 mix.7
  (28 shorter events, 1.7 us)
Async XLA Ops:
  0.6 154.7 %collective-permute-start.6 = (bf16[2048,512]{1,0:T(8,128)(2,1)}, bf16[2048,512]{1,0:T(8,128)(2,1)S(1)}, u32[]{:S(2)}, u32[]{:S(2)}) collective-permute-start(bf16[2048,512]{1,0:T(8,128)(2,1)} %bitcast.25), channel_id=1, source_target_pairs={{0,16},{2,18},{4,20},{6,22},{8,24},{10,26},{12,28},{14,30},{16,0},... | collective-permute-start | bytes 6291464 | tf_op jit(solution)/shard_map/ppermute | solution.py:37
  4.7 16.3 %copy-start.3 = (bf16[2048,512]{1,0:T(8,128)(2,1)S(1)}, bf16[2048,512]{1,0:T(8,128)(2,1)}, u32[]{:S(2)}) copy-start(bf16[2048,512]{1,0:T(8,128)(2,1)} %get-tuple-element.17) | copy-start | bytes 6291460 | tf_op jit(solution)/shard_map/cond
  6.2 17.4 %copy-start.4 = (bf16[128,2048]{1,0:T(8,128)(2,1)}, bf16[128,2048]{1,0:T(8,128)(2,1)S(1)}, u32[]{:S(2)}) copy-start(bf16[128,2048]{1,0:T(8,128)(2,1)S(1)} %get-tuple-element.76) | copy-start | bytes 1572868 | tf_op jit(solution)/shard_map/cond
  6.2 14.9 %collective-permute-start = (bf16[128,2048]{1,0:T(8,128)(2,1)S(1)}, bf16[128,2048]{1,0:T(8,128)(2,1)S(1)}, u32[]{:S(2)}, u32[]{:S(2)}) collective-permute-start(bf16[128,2048]{1,0:T(8,128)(2,1)S(1)} %get-tuple-element.70), channel_id=1, source_target_pairs={{0,1},{1,0},{2,3},{3,2},{4,5},{5,4},{6,7},{7,6},{8,9},{9,8},{10,11... | collective-permute-start | bytes 1572872 | tf_op jit(solution)/shard_map/cond/branch_1_fun/ppermute | solution.py:32
  7.8 21.9 %collective-permute-start.1 = (bf16[128,512]{1,0:T(8,128)(2,1)}, bf16[128,512]{1,0:T(8,128)(2,1)S(1)}, u32[]{:S(2)}, u32[]{:S(2)}) collective-permute-start(bf16[128,512]{1,0:T(8,128)(2,1)} %bitcast.35), channel_id=1, source_target_pairs={{0,1},{1,0},{2,3},{3,2},{4,5},{5,4},{6,7},{7,6},{8,9},{9,8},{10,11... | collective-permute-start | bytes 393224 | tf_op jit(solution)/shard_map/cond/branch_1_fun/ppermute | solution.py:32
  21.0 2.5 %copy-start.6 = (bf16[128,2048]{1,0:T(8,128)(2,1)}, bf16[128,2048]{1,0:T(8,128)(2,1)S(1)}, u32[]{:S(2)}) copy-start(bf16[128,2048]{1,0:T(8,128)(2,1)S(1)} %collective-permute-done) | copy-start | bytes 1572868 | tf_op jit(solution)/shard_map/cond
  21.5 8.2 %copy-start.9 = (bf16[1,128,2048]{2,1,0:T(8,128)(2,1)S(1)}, bf16[1,128,2048]{2,1,0:T(8,128)(2,1)}, u32[]{:S(2)}) copy-start(bf16[1,128,2048]{2,1,0:T(8,128)(2,1)} %get-tuple-element.67) | copy-start | bytes 1572868 | tf_op jit(solution)/shard_map/cond
  21.5 8.2 %copy-start.10 = (bf16[1,128,512]{2,1,0:T(8,128)(2,1)S(1)}, bf16[1,128,512]{2,1,0:T(8,128)(2,1)}, u32[]{:S(2)}) copy-start(bf16[1,128,512]{2,1,0:T(8,128)(2,1)} %get-tuple-element.68) | copy-start | bytes 393220 | tf_op jit(solution)/shard_map/cond
  21.5 6.5 %collective-permute-start.2 = (f32[128,512]{1,0:T(8,128)S(1)}, f32[128,512]{1,0:T(8,128)S(1)}, u32[]{:S(2)}, u32[]{:S(2)}) collective-permute-start(f32[128,512]{1,0:T(8,128)S(1)} %fusion.1), channel_id=1, source_target_pairs={{0,1},{1,0},{2,3},{3,2},{4,5},{5,4},{6,7},{7,6},{8,9},{9,8},{10,11... | collective-permute-start | bytes 786440 | tf_op jit(solution)/shard_map/cond/branch_1_fun/ppermute | solution.py:32
  23.1 10.0 %copy-start.8 = (bf16[1,128,2048]{2,1,0:T(8,128)(2,1)S(1)}, bf16[1,128,2048]{2,1,0:T(8,128)(2,1)}, u32[]{:S(2)}) copy-start(bf16[1,128,2048]{2,1,0:T(8,128)(2,1)} %get-tuple-element.69) | copy-start | bytes 1572868 | tf_op jit(solution)/shard_map/cond
  28.1 5.0 %collective-permute-start.3 = (bf16[128,512]{1,0:T(8,128)(2,1)S(1)}, bf16[128,512]{1,0:T(8,128)(2,1)S(1)}, u32[]{:S(2)}, u32[]{:S(2)}) collective-permute-start(bf16[128,512]{1,0:T(8,128)(2,1)S(1)} %multiply_convert_fusion.refs_0_), channel_id=1, source_target_pairs={{0,1},{1,0},{2,3},{3,2},{4,5},{5,4},{6,7},{7,6},{8,9},{9,8},{10,11... | collective-permute-start | bytes 393224 | tf_op jit(solution)/shard_map/cond/branch_1_fun/ppermute | solution.py:32
  29.7 18.8 %copy-start.5 = (bf16[128,2048]{1,0:T(8,128)(2,1)S(1)}, bf16[128,2048]{1,0:T(8,128)(2,1)}, u32[]{:S(2)}) copy-start(bf16[128,2048]{1,0:T(8,128)(2,1)} %copy-done.4) | copy-start | bytes 1572868 | tf_op jit(solution)/shard_map/cond
  29.7 18.8 %copy-start.7 = (bf16[128,2048]{1,0:T(8,128)(2,1)S(1)}, bf16[128,2048]{1,0:T(8,128)(2,1)}, u32[]{:S(2)}) copy-start(bf16[128,2048]{1,0:T(8,128)(2,1)} %copy-done.6) | copy-start | bytes 1572868 | tf_op jit(solution)/shard_map/cond
  35.2 7.3 %collective-permute-start.4 = (f32[128,512]{1,0:T(8,128)S(1)}, f32[128,512]{1,0:T(8,128)S(1)}, u32[]{:S(2)}, u32[]{:S(2)}) collective-permute-start(f32[128,512]{1,0:T(8,128)S(1)} %get-tuple-element.19), channel_id=1, source_target_pairs={{0,1},{1,0},{2,3},{3,2},{4,5},{5,4},{6,7},{7,6},{8,9},{9,8},{10,11... | collective-permute-start | bytes 786440 | tf_op jit(solution)/shard_map/cond/branch_1_fun/ppermute | solution.py:32
  43.2 5.4 %collective-permute-start.5 = (bf16[128,512]{1,0:T(8,128)(2,1)}, bf16[128,512]{1,0:T(8,128)(2,1)}, u32[]{:S(2)}, u32[]{:S(2)}) collective-permute-start(bf16[128,512]{1,0:T(8,128)(2,1)} %add_convert_fusion), channel_id=1, source_target_pairs={{0,1},{1,0},{2,3},{3,2},{4,5},{5,4},{6,7},{7,6},{8,9},{9,8},{10,11... | collective-permute-start | bytes 393224 | tf_op jit(solution)/shard_map/cond/branch_1_fun/ppermute | solution.py:32
  48.5 1.6 copy-start
  50.1 1.6 copy-start.1
  54.2 101.1 %collective-permute-start.10 = (bf16[640,512]{1,0:T(8,128)(2,1)S(1)}, bf16[640,512]{1,0:T(8,128)(2,1)S(1)}, u32[]{:S(2)}, u32[]{:S(2)}) collective-permute-start(bf16[640,512]{1,0:T(8,128)(2,1)S(1)} %get-tuple-element.53), channel_id=1, source_target_pairs={{0,16},{2,18},{4,20},{6,22},{8,24},{10,26},{12,28},{14,30},{16,0},... | collective-permute-start | bytes 1966088 | tf_op jit(solution)/shard_map/ppermute | solution.py:37
  56.8 112.6 %collective-permute-start.9 = (bf16[640,512]{1,0:T(8,128)(2,1)S(1)}, bf16[640,512]{1,0:T(8,128)(2,1)S(1)}, u32[]{:S(2)}, u32[]{:S(2)}) collective-permute-start(bf16[640,512]{1,0:T(8,128)(2,1)S(1)} %get-tuple-element.51), channel_id=1, source_target_pairs={{0,16},{2,18},{4,20},{6,22},{8,24},{10,26},{12,28},{14,30},{16,0},... | collective-permute-start | bytes 1966088 | tf_op jit(solution)/shard_map/ppermute | solution.py:37
  62.2 93.1 %copy-start.2 = (bf16[1,2048,512]{2,1,0:T(8,128)(2,1)S(1)}, bf16[1,2048,512]{2,1,0:T(8,128)(2,1)}, u32[]{:S(2)}) copy-start(bf16[1,2048,512]{2,1,0:T(8,128)(2,1)} %param.13) | copy-start | bytes 6291460
  62.2 121.2 %collective-permute-start.8 = (bf16[640,512]{1,0:T(8,128)(2,1)S(1)}, bf16[640,512]{1,0:T(8,128)(2,1)S(1)}, u32[]{:S(2)}, u32[]{:S(2)}) collective-permute-start(bf16[640,512]{1,0:T(8,128)(2,1)S(1)} %get-tuple-element.49), channel_id=1, source_target_pairs={{0,16},{2,18},{4,20},{6,22},{8,24},{10,26},{12,28},{14,30},{16,0},... | collective-permute-start | bytes 1966088 | tf_op jit(solution)/shard_map/ppermute | solution.py:37
  63.7 121.7 %collective-permute-start.7 = (bf16[128,512]{1,0:T(8,128)(2,1)S(1)}, bf16[128,512]{1,0:T(8,128)(2,1)S(1)}, u32[]{:S(2)}, u32[]{:S(2)}) collective-permute-start(bf16[128,512]{1,0:T(8,128)(2,1)S(1)} %get-tuple-element.47), channel_id=1, source_target_pairs={{0,16},{2,18},{4,20},{6,22},{8,24},{10,26},{12,28},{14,30},{16,0},... | collective-permute-start | bytes 393224 | tf_op jit(solution)/shard_map/ppermute | solution.py:37
